TPU v7x, 1024 devices: a whole 8x8x8 slice. The times are simulated.
1024 devices in a mesh: row: 64 (over z, y_hi, core), col: 16 (over y_lo, x).
Axes of the slice: x: 8, y: 8 (y_hi: 4, y_lo: 2; y = y_hi * 2 + y_lo), z: 8, core: 2. Of those that a mesh axis runs over, the one named last changes fastest.
Arguments:
- pair_elems: bfloat16 [1024, 2, 20480], P(('row', 'col')), may hold values from -3.171875 to 3.171875
- slot_pair: int32 [1024], replicated, may hold values from 0 to 1023, each once
- val_index: int32 [1024], replicated, may hold values from 0 to 2047
- cond_index: int32 [1024], replicated, may hold values from 0 to 2047
- val_energy: float32 [2048], replicated, may hold values from -12 to -1
- cond_energy: float32 [2048], replicated, may hold values from 0.5 to 10
Outputs:
- chi_zero: float32 [2, 20480, 20480], P(None, 'row', 'col')
Inputs may be any that keep to these rules, and one draw needn't show every extreme that they name: `slot_pair`: each pair is held by exactly one slot.
All inputs are finite; a program needn't handle non-finite values.
Results may differ from a plain program's by a relative error of at most 0.0028.
Values may be sent and summed in bfloat16 or wider, within the bound.
No kernel may reach another device: no remote copies, remote signals or barrier semaphores. Data moves between devices by JAX's collectives and lax.ppermute only.
A program may use at most 64 MiB of HBM per device.

v0:
```python
import jax
import jax.numpy as jnp
from jax import lax
from jax.sharding import PartitionSpec as P


def products(left_block, right_block):
    dims = (((0,), (0,)), ((), ()))
    count = left_block.shape[0]
    width = left_block.shape[2]
    col_width = right_block.shape[2]
    real_part = lax.dot_general(
        left_block.reshape(count * 2, width),
        right_block.reshape(count * 2, col_width),
        dims,
        preferred_element_type=jnp.float32,
    )
    imag_part = lax.dot_general(
        left_block[:, 1], right_block[:, 0], dims, preferred_element_type=jnp.float32
    )
    imag_part = imag_part - lax.dot_general(
        left_block[:, 0], right_block[:, 1], dims, preferred_element_type=jnp.float32
    )
    return (real_part, imag_part)


def local(pair_elems, slot_pair, val_index, cond_index, val_energy, cond_energy):
    per_dev = pair_elems.shape[0]
    full_width = pair_elems.shape[2]
    n_row = lax.axis_size("row")
    n_col = lax.axis_size("col")
    linear = lax.axis_index("row") * n_col + lax.axis_index("col")
    owner = lax.dynamic_slice_in_dim(slot_pair, linear * per_dev, per_dev, 0)
    upper = jnp.take(val_energy, jnp.take(val_index, owner))
    lower = jnp.take(cond_energy, jnp.take(cond_index, owner))
    weight = 2.0 / (upper - lower)
    dense = pair_elems.reshape(per_dev, 2 * full_width // 128, 128)
    scaled = (weight[:, None, None] * dense).astype(jnp.bfloat16).reshape(per_dev, 2, full_width)
    mine = lax.all_to_all(scaled, "row", split_axis=2, concat_axis=0, tiled=True)
    spread = lax.all_gather(mine, "col", axis=0, tiled=True)
    width = spread.shape[2]
    spread = spread.reshape(n_col, n_row, per_dev, 2, width)
    left_rows = jnp.transpose(spread, (1, 0, 2, 3, 4)).reshape(n_row * n_col * per_dev, 2, width)
    width = left_rows.shape[2]
    col_mine = lax.all_to_all(pair_elems, "col", split_axis=2, concat_axis=0, tiled=True)
    gathered = lax.all_gather(col_mine, "row", axis=0, tiled=True)
    real_part, imag_part = products(left_rows, gathered)
    return jnp.stack([real_part, imag_part])


def solution(mesh):
    in_specs = (P(("row", "col"), None, None), P(), P(), P(), P(), P())
    out_specs = P(None, "row", "col")
    return jax.shard_map(local, mesh=mesh, in_specs=in_specs, out_specs=out_specs, check_vma=False)
```

profile of v0, /device:TPU:1, one launch (start us, length us, event | category | flops | bytes accessed | tf_op | source)
XLA Modules:
  0.0 544.2 jit_solution(1703317625672704406)
XLA Ops:
  6.5 0.0 all-gather.5.cloned.1.call-start
  6.5 1.3 dynamic_slice.3
  9.8 1.3 dynamic-slice.10
  11.1 1.3 dynamic-slice.8
  13.6 1.3 dynamic-slice.9
  14.9 1.3 dynamic-slice.11
  17.5 1.0 multiply_convert_fusion
  18.4 15.8 %copy.26 = bf16[1,2,20480]{1,0,2:T(2,128)(2,1)} copy(bf16[1,2,20480]{2,1,0:T(2,128)(2,1)S(1)} %multiply_convert_fusion) | data formatting | bytes 163840 | tf_op jit(solution)/shard_map/convert_element_type | solution.py:38
  34.3 0.6 broadcast.44
  34.8 113.0 %reduce.1 = bf16[20480,2]{1,0:T(8,128)(2,1)} reduce(bf16[20480,1,2]{2,1,0:T(2,128)(2,1)} %bitcast.47, bf16[]{:T(256)} %broadcast.44), dimensions={1}, to_apply=%bitcast.41.reduce_sub_computation | reduce | bytes 163842
  147.8 8.3 %reshape.132 = bf16[64,2,320]{2,1,0:T(2,128)(2,1)S(1)} reshape(bf16[20480,2]{1,0:T(8,128)(2,1)} %reduce.1) | data formatting | bytes 163840
  156.1 37.0 %all_to_all.36 = bf16[64,2,320]{2,1,0:T(2,128)(2,1)S(1)} all-to-all(bf16[64,2,320]{2,1,0:T(2,128)(2,1)S(1)} %reshape.132), channel_id=1, replica_groups=mesh['row'=64,'col'=16] {'row'}, dimensions={0} | all-to-all | bytes 163840 | tf_op jit(solution)/shard_map/all_to_all | solution.py:39
  193.1 18.4 %reshape.133 = bf16[20480,1,2]{2,1,0:T(2,128)(2,1)} reshape(bf16[64,2,320]{2,1,0:T(2,128)(2,1)S(1)} %all_to_all.36) | data formatting | bytes 163840
  211.5 0.0 copy-start.2
  211.5 18.9 %copy.27 = bf16[1,2,20480]{2,1,0:T(2,128)(2,1)S(1)} copy(bf16[1,2,20480]{1,0,2:T(2,128)(2,1)} %bitcast.48) | data formatting | bytes 163840 | tf_op jit(solution)/shard_map/all_to_all | solution.py:39
  230.4 0.8 all_to_all.27
  231.2 0.0 all-gather.5.cloned.1.call-update
  231.2 0.2 all-gather.7.cloned.1.call-start
  231.5 0.0 copy-done.2
  231.5 15.8 %copy.29 = bf16[1,2,20480]{1,0,2:T(2,128)(2,1)} copy(bf16[1,2,20480]{2,1,0:T(2,128)(2,1)S(1)} %copy-done.2) | data formatting | bytes 163840 | tf_op args[0]
  247.3 113.0 %reduce = bf16[20480,2]{1,0:T(8,128)(2,1)} reduce(bf16[20480,1,2]{2,1,0:T(2,128)(2,1)} %bitcast.49, bf16[]{:T(256)} %broadcast.44), dimensions={1}, to_apply=%bitcast.39.reduce_sub_computation | reduce | bytes 163842
  360.3 9.3 %reshape.130 = bf16[16,2,1280]{2,1,0:T(2,128)(2,1)S(1)} reshape(bf16[20480,2]{1,0:T(8,128)(2,1)} %reduce) | data formatting | bytes 163840
  369.6 14.2 %all_to_all.37 = bf16[16,2,1280]{2,1,0:T(2,128)(2,1)S(1)} all-to-all(bf16[16,2,1280]{2,1,0:T(2,128)(2,1)S(1)} %reshape.130), channel_id=1, replica_groups=mesh['row'=64,'col'=16] {'col'}, dimensions={0} | all-to-all | bytes 163840 | tf_op jit(solution)/shard_map/all_to_all | solution.py:45
  383.8 13.5 %reshape.131 = bf16[20480,1,2]{2,1,0:T(2,128)(2,1)} reshape(bf16[16,2,1280]{2,1,0:T(2,128)(2,1)S(1)} %all_to_all.37) | data formatting | bytes 163840
  397.3 18.9 %copy.30 = bf16[1,2,20480]{2,1,0:T(2,128)(2,1)S(1)} copy(bf16[1,2,20480]{1,0,2:T(2,128)(2,1)} %bitcast.50) | data formatting | bytes 163840 | tf_op jit(solution)/shard_map/all_to_all | solution.py:45
  416.2 0.7 copy.37
  416.9 0.0 all-gather.7.cloned.1.call-update
  416.9 0.0 all-gather.5.cloned.1.call-done
  416.9 0.0 copy-start.1
  416.9 3.6 copy.32
  420.5 0.0 copy-done.1
  420.5 1.6 copy.28
  422.1 1.3 reshape_reshape.3
  423.5 80.0 %all-gather.7.cloned.1.call-done = bf16[1024,1,2,1280]{3,0,2,1:T(8,128)(2,1)} async-done(((bf16[16,1,2,1280]{3,0,2,1:T(8,128)(2,1)}), bf16[1024,1,2,1280]{3,0,2,1:T(8,128)(2,1)}) %all-gather.7.cloned.1.call-update) | async-done | bytes 5242896 | tf_op jit(solution)/shard_map/all_gather | solution.py:46
  503.5 0.0 copy-start
  503.5 3.2 fusion.1
  506.6 0.3 copy-done
  507.0 2.2 fusion
  509.2 10.2 %copy.31 = bf16[1024,1,2,1280]{3,2,0,1:T(2,128)(2,1)} copy(bf16[1024,1,2,1280]{3,0,2,1:T(8,128)(2,1)} %all-gather.7.cloned.1.call-done) | data formatting | bytes 10485760 | tf_op jit(solution)/shard_map/all_gather | solution.py:46
  519.4 11.7 %reshape.23 = bf16[2048,1280]{1,0:T(8,128)(2,1)} reshape(bf16[1024,1,2,1280]{3,2,0,1:T(2,128)(2,1)} %copy.31) | data formatting | bytes 10485760 | tf_op jit(solution)/shard_map/reshape | solution.py:14
  531.1 4.4 convolution_bitcast_fusion
  535.4 1.9 pad_maximum_fusion
Async XLA Ops:
  6.5 410.4 %all-gather.5.cloned.1.call-start = ((), (), s32[]{:S(2)}) async-start(), calls=%async_computation.2 | async-start | bytes 1671168 | tf_op jit(solution)/shard_map/all_gather | solution.py:40
  211.5 20.0 %copy-start.2 = (bf16[1,2,20480]{2,1,0:T(2,128)(2,1)S(1)}, bf16[1,2,20480]{2,1,0:T(2,128)(2,1)}, u32[]{:S(2)}) copy-start(bf16[1,2,20480]{2,1,0:T(2,128)(2,1)} %param.6) | copy-start | bytes 245764
  231.2 272.2 %all-gather.7.cloned.1.call-start = ((), (), s32[]{:S(2)}) async-start(), calls=%async_computation.3 | async-start | bytes 5324800 | tf_op jit(solution)/shard_map/all_gather | solution.py:46
  416.9 3.6 copy-start.1
  503.5 3.5 copy-start
Sparse Core Ops, SparseCore 0:
  231.4 57.3 all-gather.4
  417.0 86.4 all-gather.6
where the time goes:
time: 546 us; the launch traced here: 544 us
  other arithmetic  229 us (42%)
  local copies, waits for them, and re-layouts  156 us (29%)
  waiting for transfers between devices  80.1 us (15%)
  blocking collectives  51.2 us (9%)
  between operations  18 us (3%)
  matrix products  9.73 us (2%)
    unnamed x2, other arithmetic  226 us
    all_gather x1, waiting for transfers between devices, local(): gathered = lax.all_gather(col_mine, 'row', axis=0, tiled=True)  80 us
    unnamed x13, local copies, waits for them, and re-layouts  66.9 us
    all_to_all x1, blocking collectives, local(): lax.all_to_all(scaled, 'row', split_axis=2, concat_axis=0, tiled=True)  37 us
    all_to_all x2, local copies, waits for them, and re-layouts, local(): lax.all_to_all(scaled, 'row', split_axis=2, concat_axis=0, tiled=True)  19.7 us
    all_to_all x1, local copies, waits for them, and re-layouts, local(): lax.all_to_all(pair_elems, 'col', split_axis=2, concat_axis=0, tiled=True)  18.9 us
    convert_element_type x1, local copies, waits for them, and re-layouts, local(): (weight[:, None, None] * dense).astype(jnp.bfloat16)  15.8 us
    all_to_all x1, blocking collectives, local(): lax.all_to_all(pair_elems, 'col', split_axis=2, concat_axis=0, tiled=True)  14.2 us
  transfers between devices with their start and end apart: 2, of which 1 were waited for; matrix products, arithmetic and copies ran while one was open for 33% of the time, Pallas kernels for 0%

commit v1 on v0

v1 whole, which is shorter than its diff:
```python
import jax
import jax.numpy as jnp
from jax import lax
from jax.experimental import pallas as pl
from jax.experimental.pallas import tpu as pltpu
from jax.sharding import PartitionSpec as P

LANES = 128
BF16 = jnp.bfloat16
F32 = jnp.float32
VMEM = pl.BlockSpec(memory_space=pltpu.VMEM)
SMEM = pl.BlockSpec(memory_space=pltpu.SMEM)
LIMIT = pltpu.CompilerParams(vmem_limit_bytes=48 * 1024 * 1024)


def split_right(elems, n_col):
    width = elems.shape[2] // n_col

    def kernel(in_ref, out_ref):
        for block in range(n_col):
            out_ref[block] = in_ref[0, :, block * width : (block + 1) * width]

    return pl.pallas_call(
        kernel,
        out_shape=jax.ShapeDtypeStruct((n_col, 2, width), BF16),
        in_specs=[VMEM],
        out_specs=VMEM,
        compiler_params=LIMIT,
    )(elems)


def split_left(elems, tables, position, n_row, span):
    full = elems.shape[2]
    width = full // n_row

    def kernel(where_ref, slot_ref, val_ref, cond_ref, upper_ref, lower_ref, in_ref, out_ref):
        owner = slot_ref[where_ref[0]]
        gap = upper_ref[val_ref[owner]] - lower_ref[cond_ref[owner]]
        weight = 2.0 / jnp.full((2, LANES), gap, F32)
        for tile in range(full // LANES):
            part = in_ref[0, :, tile * LANES : (tile + 1) * LANES]
            part = (weight * part.astype(F32)).astype(BF16)
            for block in range(n_row):
                place = tile - block * width // LANES
                if 0 <= place < span // LANES:
                    out_ref[block, :, place * LANES : (place + 1) * LANES] = part

    return pl.pallas_call(
        kernel,
        out_shape=jax.ShapeDtypeStruct((n_row, 2, span), BF16),
        in_specs=[SMEM] * 6 + [VMEM],
        out_specs=VMEM,
        compiler_params=LIMIT,
    )(position, *tables, elems)


def part_rows(slots):
    count, _, width = slots.shape

    def kernel(in_ref, out_ref):
        for tile in range(width // LANES):
            cut = slice(tile * LANES, (tile + 1) * LANES)
            both = in_ref[:, :, cut].astype(F32)
            out_ref[:count, cut] = both[:, 0, :].astype(BF16)
            out_ref[count:, cut] = both[:, 1, :].astype(BF16)

    return pl.pallas_call(
        kernel,
        out_shape=jax.ShapeDtypeStruct((2 * count, width), BF16),
        in_specs=[VMEM],
        out_specs=VMEM,
        compiler_params=LIMIT,
    )(slots)


def order_left(rows, shift, n_row, n_col, width):
    depth, span = rows.shape
    group = 2 * n_col

    def kernel(shift_ref, in_ref, out_ref, real_ref, imag_ref, turn_ref):
        off = pl.multiple_of(shift_ref[0], 64)
        for col in range(n_col):
            base = col * 2 * n_row
            first = pl.ds(col, n_row, stride=group)
            second = pl.ds(n_col + col, n_row, stride=group)
            for tile in range(span // LANES):
                cut = slice(tile * LANES, (tile + 1) * LANES)
                re = in_ref[base : base + n_row, cut].astype(F32)
                im = in_ref[base + n_row : base + 2 * n_row, cut].astype(F32)
                real_ref[tile, first, :] = re
                real_ref[tile, second, :] = im
                imag_ref[tile, first, :] = im
                imag_ref[tile, second, :] = -re
        step = min(256, depth)
        for which, source in enumerate((real_ref, imag_ref)):
            for tile in range(span // LANES):
                cut = slice(tile * LANES, (tile + 1) * LANES)
                for at in range(0, depth, step):
                    turn_ref[cut, at : at + step] = source[tile, at : at + step, :].T.astype(BF16)
            out_ref[which] = turn_ref[pl.ds(off, width), :]

    return pl.pallas_call(
        kernel,
        out_shape=jax.ShapeDtypeStruct((2, width, depth), BF16),
        in_specs=[SMEM, VMEM],
        out_specs=VMEM,
        scratch_shapes=[
            pltpu.VMEM((span // LANES, depth, LANES), F32),
            pltpu.VMEM((span // LANES, depth, LANES), F32),
            pltpu.VMEM((span, depth), BF16),
        ],
        compiler_params=LIMIT,
    )(shift, rows)


def multiply(left, right):
    _, width, depth = left.shape
    columns = right.shape[1]
    step = 256

    def kernel(left_ref, right_ref, out_ref):
        for which in range(2):
            out_ref[which] = jnp.dot(left_ref[which], right_ref[...], preferred_element_type=F32)

    return pl.pallas_call(
        kernel,
        grid=(columns // step,),
        out_shape=jax.ShapeDtypeStruct((2, width, columns), F32),
        in_specs=[
            pl.BlockSpec((2, width, depth), lambda j: (0, 0, 0)),
            pl.BlockSpec((depth, step), lambda j: (0, j)),
        ],
        out_specs=pl.BlockSpec((2, width, step), lambda j: (0, 0, j)),
        compiler_params=LIMIT,
        cost_estimate=pl.CostEstimate(
            flops=4 * width * depth * columns,
            bytes_accessed=2 * depth * (2 * width + columns) + 8 * width * columns,
            transcendentals=0,
        ),
    )(left, right)


def local(pair_elems, slot_pair, val_index, cond_index, val_energy, cond_energy):
    full = pair_elems.shape[2]
    n_row = lax.axis_size("row")
    n_col = lax.axis_size("col")
    row = lax.axis_index("row")
    position = (row * n_col + lax.axis_index("col")).astype(jnp.int32).reshape(1)
    width = full // n_row
    span = 3 * LANES

    right = split_right(pair_elems, n_col)
    right = lax.all_to_all(right, "col", split_axis=0, concat_axis=0, tiled=True)
    right = lax.all_gather(part_rows(right), "row", axis=0, tiled=True)

    tables = (slot_pair, val_index, cond_index, val_energy, cond_energy)
    left = split_left(pair_elems, tables, position, n_row, span)
    left = lax.all_to_all(left, "row", split_axis=0, concat_axis=0, tiled=True)
    left = part_rows(left)
    left = jnp.broadcast_to(left[None], (n_col, *left.shape))
    left = lax.all_to_all(left, "col", split_axis=0, concat_axis=0, tiled=True)
    left = left.reshape(n_col * left.shape[1], span)
    shift = (lax.rem(row * width, LANES)).astype(jnp.int32).reshape(1)
    left = order_left(left, shift, n_row, n_col, width)
    return multiply(left, right)


def solution(mesh):
    in_specs = (P(("row", "col"), None, None), P(), P(), P(), P(), P())
    out_specs = P(None, "row", "col")
    return jax.shard_map(local, mesh=mesh, in_specs=in_specs, out_specs=out_specs, check_vma=False)
```

time: 546 us -> 151 us (0.28)
  other arithmetic: 229 us -> 0 us
  local copies, waits for them, and re-layouts: 156 us -> 9.79 us
  waiting for transfers between devices: 80.1 us -> 54.4 us
  Pallas kernels: 0 us -> 13.9 us
  matrix products: 9.73 us -> 0 us
    unnamed x2 -> x0, other arithmetic: 226 us -> none
    all_gather x2 -> x1, waiting for transfers between devices: 80 us -> 17.4 us  [local(): right = lax.all_gather(part_rows(right), 'row', axis=0, tiled=True)]
    unnamed x13 -> x18, local copies, waits for them, and re-layouts: 66.9 us -> 8.45 us
    all_to_all x3 -> x0, local copies, waits for them, and re-layouts: 38.6 us -> none  [the longest x2 19.7 us: local(): lax.all_to_all(scaled, 'row', split_axis=2, concat_axis=0, tiled=True)]
    all_to_all x0 -> x1, waiting for transfers between devices: none -> 37 us  [local(): left = lax.all_to_all(left, 'col', split_axis=0, concat_axis=0, tiled=True)]
    convert_element_type x1 -> x0, local copies, waits for them, and re-layouts: 15.8 us -> none  [local(): (weight[:, None, None] * dense).astype(jnp.bfloat16)]
    pallas_call x0 -> x6, Pallas kernels: none -> 13.9 us  [the longest x1 7.55 us: multiply(): pl.pallas_call(kernel, grid=(columns // step,), out_shape=jax.ShapeDtypeS...]
    reshape x1 -> x0, local copies, waits for them, and re-layouts: 11.7 us -> none  [products(): right_block.reshape(count * 2, col_width)]
  transfers between devices with their start and end apart: 2 -> 2, of which waited for: 1 -> 2; matrix products, arithmetic and copies ran while one was open for 33% -> 1% of each run, Pallas kernels for 0% -> 4%
where the time goes in v1:
time: 151 us; the launch traced here: 148 us
  waiting for transfers between devices  54.4 us (36%)
  blocking collectives  53.1 us (35%)
  Pallas kernels  13.9 us (9%)
  between operations  13.5 us (9%)
  local copies, waits for them, and re-layouts  9.79 us (6%)
  starting transfers between devices  3.71 us (2%)
    all_to_all x1, blocking collectives, local(): left = lax.all_to_all(left, 'row', split_axis=0, concat_axis=0, tiled=True)  37.3 us
    all_to_all x1, waiting for transfers between devices, local(): left = lax.all_to_all(left, 'col', split_axis=0, concat_axis=0, tiled=True)  37 us
    all_gather x1, waiting for transfers between devices, local(): right = lax.all_gather(part_rows(right), 'row', axis=0, tiled=True)  17.4 us
    all_to_all x1, blocking collectives, local(): lax.all_to_all(right, 'col', split_axis=0, concat_axis=0, tiled=True)  15.7 us
    unnamed x18, local copies, waits for them, and re-layouts  8.45 us
    pallas_call x1, Pallas kernels, multiply(): pl.pallas_call(kernel, grid=(columns // step,), out_shape=jax.ShapeDtypeS...  7.55 us
    pallas_call x1, Pallas kernels, order_left(): pl.pallas_call(kernel, out_shape=jax.ShapeDtypeStruct((2, width, depth),...  4.33 us
    all_to_all x1, starting transfers between devices, local(): left = lax.all_to_all(left, 'col', split_axis=0, concat_axis=0, tiled=True)  3.71 us
  transfers between devices with their start and end apart: 2, of which 2 were waited for; matrix products, arithmetic and copies ran while one was open for 1% of the time, Pallas kernels for 4%

profile of v1, /device:TPU:1, one launch (start us, length us, event | category | flops | bytes accessed | tf_op | source)
XLA Modules:
  0.0 148.3 jit_solution(9414897242437630631)
XLA Ops:
  6.5 0.0 all-gather.2.cloned.1.call-start
  6.5 0.0 copy-start.2
  6.5 0.9 copy-done.2
  7.4 15.7 %all_to_all.15.in_ref = bf16[16,2,1280]{2,1,0:T(2,128)(2,1)S(1)} all-to-all(bf16[16,2,1280]{2,1,0:T(2,128)(2,1)S(1)} %shard_map.67), channel_id=1, replica_groups=mesh['row'=64,'col'=16] {'col'}, dimensions={0} | all-to-all | bytes 163840 | tf_op jit(solution)/shard_map/all_to_all | solution.py:153
  23.2 0.7 shard_map.68
  23.9 0.0 all-gather.2.cloned.1.call-update
  23.9 0.0 copy-start.3
  23.9 0.9 copy-done.3
  24.8 0.0 copy-start.4
  24.8 0.7 copy-done.4
  25.5 0.0 copy-start.5
  25.5 0.7 copy-done.5
  26.2 0.0 copy-start.6
  26.2 0.7 copy-done.6
  26.9 0.0 copy-start.7
  26.9 0.7 copy-done.7
  27.6 0.0 copy-start.8
  27.6 0.7 copy-done.8
  28.3 1.1 shard_map.64
  29.4 37.3 %all_to_all.16.in_ref = bf16[64,2,384]{2,1,0:T(2,128)(2,1)S(1)} all-to-all(bf16[64,2,384]{2,1,0:T(2,128)(2,1)S(1)} %shard_map.64), channel_id=1, replica_groups=mesh['row'=64,'col'=16] {'row'}, dimensions={0} | all-to-all | bytes 196608 | tf_op jit(solution)/shard_map/all_to_all | solution.py:158
  66.7 0.2 shard_map.65
  66.9 1.3 broadcast_in_dim.2
  68.2 3.7 %all-to-all-start.1 = ((bf16[16,128,384]{2,1,0:T(8,128)(2,1)}), bf16[16,128,384]{2,1,0:T(8,128)(2,1)S(1)}, u32[]{:S(2)}, u32[]{:S(2)}) async-start(bf16[16,128,384]{2,1,0:T(8,128)(2,1)} %broadcast_in_dim.2), calls=%async_computation.1 | async-start | bytes 3145728 | tf_op jit(solution)/shard_map/all_to_all | solution.py:161
  72.0 37.0 %all-to-all-done.1 = bf16[16,128,384]{2,1,0:T(8,128)(2,1)S(1)} async-done(((bf16[16,128,384]{2,1,0:T(8,128)(2,1)}), bf16[16,128,384]{2,1,0:T(8,128)(2,1)S(1)}, u32[]{:S(2)}, u32[]{:S(2)}) %all-to-all-start.1) | async-done | bytes 1572896 | tf_op jit(solution)/shard_map/all_to_all | solution.py:161
  109.0 4.3 %shard_map.66.left_ref = bf16[2,320,2048]{2,1,0:T(8,128)(2,1)S(1)} custom-call(s32[1]{0:T(128)} %bitcast.shift_ref, bf16[2048,384]{1,0:T(8,128)(2,1)S(1)} %bitcast.3), custom_call_target="tpu_custom_call" | custom-call | tf_op jit(solution)/shard_map/pallas_call | solution.py:102
  113.3 0.0 copy-start
  113.3 1.5 copy-done
  114.8 17.4 %all-gather.2.cloned.1.call-done.right_ref = bf16[2048,1280]{1,0:T(8,128)(2,1)} async-done(((bf16[32,1280]{1,0:T(8,128)(2,1)}), bf16[2048,1280]{1,0:T(8,128)(2,1)}) %all-gather.2.cloned.1.call-update) | async-done | bytes 5242896 | tf_op jit(solution)/shard_map/all_gather | solution.py:154
  132.2 0.0 copy-start.1
  132.2 1.7 %copy-done.1 = bf16[2,320,2048]{2,1,0:T(8,128)(2,1)S(1)} copy-done((bf16[2,320,2048]{2,1,0:T(8,128)(2,1)S(1)}, bf16[2,320,2048]{2,1,0:T(8,128)(2,1)}, u32[]{:S(2)}) %copy-start.1) | copy-done | bytes 2621464
  133.9 7.5 %shard_map.69 = f32[2,320,1280]{2,1,0:T(8,128)} custom-call(bf16[2,320,2048]{2,1,0:T(8,128)(2,1)S(1)} %copy-done.1, bf16[2048,1280]{1,0:T(8,128)(2,1)} %all-gather.2.cloned.1.call-done.right_ref), custom_call_target="tpu_custom_call" | custom-call | flops 3355443200 | bytes 11141120 | tf_op jit(solution)/shard_map/pallas_call | solution.py:125
  (1 shorter events, 0.0 us)
Async XLA Ops:
  6.5 125.6 %all-gather.2.cloned.1.call-start = ((), (), s32[]{:S(2)}) async-start(), calls=%async_computation.3 | async-start | bytes 5324800 | tf_op jit(solution)/shard_map/all_gather | solution.py:154
  6.5 0.9 copy-start.2
  23.9 0.9 copy-start.3
  24.8 0.7 copy-start.4
  25.5 0.7 copy-start.5
  26.2 0.7 copy-start.6
  26.9 0.7 copy-start.7
  27.6 0.7 copy-start.8
  68.2 40.7 %all-to-all-start.1 = ((bf16[16,128,384]{2,1,0:T(8,128)(2,1)}), bf16[16,128,384]{2,1,0:T(8,128)(2,1)S(1)}, u32[]{:S(2)}, u32[]{:S(2)}) async-start(bf16[16,128,384]{2,1,0:T(8,128)(2,1)} %broadcast_in_dim.2), calls=%async_computation.1 | async-start | bytes 3145728 | tf_op jit(solution)/shard_map/all_to_all | solution.py:161
  113.3 1.5 %copy-start = (bf16[2,320,2048]{2,1,0:T(8,128)(2,1)}, bf16[2,320,2048]{2,1,0:T(8,128)(2,1)S(1)}, u32[]{:S(2)}) copy-start(bf16[2,320,2048]{2,1,0:T(8,128)(2,1)S(1)} %shard_map.66.left_ref) | copy-start | bytes 7864324
  132.2 1.7 %copy-start.1 = (bf16[2,320,2048]{2,1,0:T(8,128)(2,1)S(1)}, bf16[2,320,2048]{2,1,0:T(8,128)(2,1)}, u32[]{:S(2)}) copy-start(bf16[2,320,2048]{2,1,0:T(8,128)(2,1)} %copy-done) | copy-start | bytes 7864324
Sparse Core Ops, SparseCore 0:
  24.0 108.0 all-gather.1

commit v2 on v1

v2 whole, which is shorter than its diff:
```python
import jax
import jax.numpy as jnp
from jax import lax
from jax.experimental import pallas as pl
from jax.experimental.pallas import tpu as pltpu
from jax.sharding import Mesh
from jax.sharding import PartitionSpec as P

LANES = 128
ROW = ("z", "yh", "core")
COL = ("yl", "x")
BF16 = jnp.bfloat16
F32 = jnp.float32
VMEM = pl.BlockSpec(memory_space=pltpu.VMEM)
SMEM = pl.BlockSpec(memory_space=pltpu.SMEM)
LIMIT = pltpu.CompilerParams(vmem_limit_bytes=48 * 1024 * 1024)
WHOLE = pltpu.CompilerParams(vmem_limit_bytes=60 * 1024 * 1024)


def split_right(elems, n_col):
    width = elems.shape[2] // n_col

    def kernel(in_ref, out_ref):
        for block in range(n_col):
            out_ref[block] = in_ref[0, :, block * width : (block + 1) * width]

    return pl.pallas_call(
        kernel,
        out_shape=jax.ShapeDtypeStruct((n_col, 2, width), BF16),
        in_specs=[VMEM],
        out_specs=VMEM,
        compiler_params=WHOLE,
    )(elems)


def split_left(elems, tables, position, n_row, span, place_of):
    full = elems.shape[2]
    width = full // n_row

    def kernel(where_ref, slot_ref, val_ref, cond_ref, upper_ref, lower_ref, in_ref, out_ref):
        owner = slot_ref[where_ref[0]]
        gap = upper_ref[val_ref[owner]] - lower_ref[cond_ref[owner]]
        weight = 2.0 / jnp.full((2, LANES), gap, F32)
        for tile in range(full // LANES):
            part = in_ref[0, :, tile * LANES : (tile + 1) * LANES]
            part = (weight * part.astype(F32)).astype(BF16)
            for block in range(n_row):
                place = tile - block * width // LANES
                if 0 <= place < span // LANES:
                    slab = place_of(block)
                    out_ref[slab, :, place * LANES : (place + 1) * LANES] = part

    return pl.pallas_call(
        kernel,
        out_shape=jax.ShapeDtypeStruct((n_row, 2, span), BF16),
        in_specs=[SMEM] * 6 + [VMEM],
        out_specs=VMEM,
        compiler_params=WHOLE,
    )(position, *tables, elems)


def part_rows(slots):
    count, _, width = slots.shape

    def kernel(in_ref, out_ref):
        for tile in range(width // LANES):
            cut = slice(tile * LANES, (tile + 1) * LANES)
            both = in_ref[:, :, cut].astype(F32)
            out_ref[:count, cut] = both[:, 0, :].astype(BF16)
            out_ref[count:, cut] = both[:, 1, :].astype(BF16)

    return pl.pallas_call(
        kernel,
        out_shape=jax.ShapeDtypeStruct((2 * count, width), BF16),
        in_specs=[VMEM],
        out_specs=VMEM,
        compiler_params=LIMIT,
    )(slots)


def pack_left(slots, shift):
    count = slots.shape[0]
    half = LANES // 2

    def kernel(shift_ref, in_ref, out_ref):
        low = lax.broadcasted_iota(jnp.int32, (count, LANES), 1) < half
        moved = jnp.full((count, LANES), shift_ref[0], jnp.int32) > 0
        tiles = [in_ref[:, :, t * LANES : (t + 1) * LANES].astype(F32) for t in range(3)]
        ends = []
        for part in range(2):
            now = [tile[:, part, :] for tile in tiles]
            swapped = [pltpu.roll(tile, half, 1) for tile in now]
            for t in range(2):
                ahead = jnp.where(low, swapped[t], swapped[t + 1])
                slab = 2 * part + t
                out_ref[slab * count : (slab + 1) * count, :] = jnp.where(moved, ahead, now[t]).astype(BF16)
            ends.append(jnp.where(moved, swapped[2], now[2]))
        out_ref[4 * count :, :] = jnp.where(low, ends[0], pltpu.roll(ends[1], half, 1)).astype(BF16)

    return pl.pallas_call(
        kernel,
        out_shape=jax.ShapeDtypeStruct((5 * count, LANES), BF16),
        in_specs=[SMEM, VMEM],
        out_specs=VMEM,
        compiler_params=LIMIT,
    )(shift, slots)


def order_left(slabs, n_row, n_col, width):
    depth = 2 * n_row * n_col
    half = LANES // 2
    slots = 5 * n_row

    def kernel(in_ref, out_ref, real_ref, imag_ref):
        for col in range(n_col):
            first = pl.ds(col, n_row, stride=2 * n_col)
            second = pl.ds(n_col + col, n_row, stride=2 * n_col)
            rows = []
            for slab in range(5):
                at = col * slots + slab * n_row
                rows.append(in_ref[at : at + n_row, :].astype(F32))
            rows = [(rows[0], rows[2]), (rows[1], rows[3]), (rows[4], pltpu.roll(rows[4], half, 1))]
            for tile, (re, im) in enumerate(rows):
                real_ref[tile, first, :] = re
                real_ref[tile, second, :] = im
                imag_ref[tile, first, :] = im
                imag_ref[tile, second, :] = -re
        step = min(256, depth)
        for which, source in enumerate((real_ref, imag_ref)):
            for tile in range(3):
                keep = min(LANES, width - tile * LANES)
                for at in range(0, depth, step):
                    turned = source[tile, at : at + step, :].T.astype(BF16)
                    out_ref[which, tile * LANES : tile * LANES + keep, at : at + step] = turned[:keep]

    return pl.pallas_call(
        kernel,
        out_shape=jax.ShapeDtypeStruct((2, width, depth), BF16),
        in_specs=[VMEM],
        out_specs=VMEM,
        scratch_shapes=[pltpu.VMEM((3, depth, LANES), F32), pltpu.VMEM((3, depth, LANES), F32)],
        compiler_params=LIMIT,
    )(slabs)


def multiply(half, left, right, total=None):
    depth, columns = right.shape
    width = left.shape[1]
    step = 256

    def kernel(half_ref, left_ref, right_ref, *refs):
        out_ref = refs[-1]
        for which in range(2):
            product = jnp.dot(left_ref[which], right_ref[...], preferred_element_type=F32)
            out_ref[which] = product if total is None else refs[0][which] + product

    out_spec = pl.BlockSpec((2, width, step), lambda j, half_ref: (0, 0, j))
    extra = [] if total is None else [total]
    return pl.pallas_call(
        kernel,
        grid_spec=pltpu.PrefetchScalarGridSpec(
            num_scalar_prefetch=1,
            grid=(columns // step,),
            in_specs=[
                pl.BlockSpec((2, width, depth), lambda j, half_ref: (0, 0, half_ref[0])),
                pl.BlockSpec((depth, step), lambda j, half_ref: (0, j)),
            ]
            + [out_spec] * len(extra),
            out_specs=out_spec,
        ),
        out_shape=jax.ShapeDtypeStruct((2, width, columns), F32),
        input_output_aliases={3: 0} if extra else {},
        compiler_params=LIMIT,
        cost_estimate=pl.CostEstimate(
            flops=4 * width * depth * columns,
            bytes_accessed=2 * depth * (2 * width + columns) + 8 * width * columns,
            transcendentals=0,
        ),
    )(half, left, right, *extra)


def local(pair_elems, slot_pair, val_index, cond_index, val_energy, cond_energy):
    full = pair_elems.shape[2]
    n_row = lax.axis_size(ROW)
    n_col = lax.axis_size(COL)
    row = lax.axis_index(ROW)
    core = lax.axis_index("core").astype(jnp.int32).reshape(1)
    position = (row * n_col + lax.axis_index(COL)).astype(jnp.int32).reshape(1)
    width = full // n_row
    span = 3 * LANES

    def place_of(block):
        return block % 2 * (n_row // 2) + block // 2

    right = split_right(pair_elems, n_col)
    right = lax.all_to_all(right, COL, split_axis=0, concat_axis=0, tiled=True)

    tables = (slot_pair, val_index, cond_index, val_energy, cond_energy)
    left = split_left(pair_elems, tables, position, n_row, span, place_of)
    left = lax.all_to_all(left, ("core", "z", "yh"), split_axis=0, concat_axis=0, tiled=True)

    right = lax.all_gather(part_rows(right), ("z", "yh"), axis=0, tiled=True)
    shift = lax.rem(row * width, LANES).astype(jnp.int32).reshape(1)
    left = pack_left(left, shift)
    left = jnp.broadcast_to(left[None], (n_col, *left.shape))
    left = lax.all_to_all(left, COL, split_axis=0, concat_axis=0, tiled=True)
    left = order_left(left.reshape(n_col * left.shape[1], LANES), n_row, n_col, width)
    right, left = lax.optimization_barrier((right, left))

    other = lax.ppermute(right, "core", [(0, 1), (1, 0)])
    total = multiply(core, left, right)
    return multiply(1 - core, left, other, total)


def solution(mesh):
    n_row, n_col = mesh.devices.shape
    torus = Mesh(mesh.devices.reshape(n_row // 8, 4, 2, 2, n_col // 2), (*ROW, *COL))
    in_specs = (P((*ROW, *COL), None, None), P(), P(), P(), P(), P())
    out_specs = P(None, ROW, COL)
    return jax.shard_map(local, mesh=torus, in_specs=in_specs, out_specs=out_specs, check_vma=False)
```

time: 151 us -> 151 us (level); the launches traced: 148 us -> 151 us
  starting transfers between devices: 3.71 us -> 28.3 us
  waiting for transfers between devices: 54.4 us -> 37.1 us
  local copies, waits for them, and re-layouts: 9.79 us -> 1.98 us
  Pallas kernels: 13.9 us -> 19.5 us
  blocking collectives: 53.1 us -> 50.6 us
    all_to_all x1, waiting for transfers between devices: 37 us -> 12.2 us  [local(): lax.all_to_all(left, ('core', 'z', 'yh'), split_axis=0, concat_axis=0, ti...]
    all_to_all x1, starting transfers between devices: 3.71 us -> 24.3 us  [local(): lax.all_to_all(left, ('core', 'z', 'yh'), split_axis=0, concat_axis=0, ti...]
    all_gather x1, waiting for transfers between devices: 17.4 us -> 24.9 us  [local(): right = lax.all_gather(part_rows(right), ('z', 'yh'), axis=0, tiled=True)]
    unnamed x18 -> x2, local copies, waits for them, and re-layouts: 8.45 us -> 1.73 us
    ppermute x0 -> x1, starting transfers between devices: none -> 4.06 us  [local(): other = lax.ppermute(right, 'core', [(0, 1), (1, 0)])]
    pallas_call x1 -> x3, Pallas kernels: 7.55 us -> 10.7 us  [the longest x2 10.4 us: multiply(): pl.pallas_call(kernel, grid_spec=pltpu.PrefetchScalarGridSpec(num_scalar_...]
    all_to_all x2, blocking collectives: 53.1 us -> 50.6 us  [the longest x1 34.6 us: local(): left = lax.all_to_all(left, COL, split_axis=0, concat_axis=0, tiled=True)]
    pallas_call x1, Pallas kernels: 0.01 us -> 1.53 us  [split_right(): pl.pallas_call(kernel, out_shape=jax.ShapeDtypeStruct((n_col, 2, width),...]
  transfers between devices with their start and end apart: 2 -> 3, of which waited for: 2 -> 2; matrix products, arithmetic and copies ran while one was open for 1% -> 0% of each run, Pallas kernels for 4% -> 7%
where the time goes in v2:
time: 151 us
  blocking collectives  50.6 us (34%)
  waiting for transfers between devices  37.1 us (25%)
  starting transfers between devices  28.3 us (19%)
  Pallas kernels  19.5 us (13%)
  between operations  13.5 us (9%)
  local copies, waits for them, and re-layouts  1.98 us (1%)
    all_to_all x1, blocking collectives, local(): left = lax.all_to_all(left, COL, split_axis=0, concat_axis=0, tiled=True)  34.6 us
    all_gather x1, waiting for transfers between devices, local(): right = lax.all_gather(part_rows(right), ('z', 'yh'), axis=0, tiled=True)  24.9 us
    all_to_all x1, starting transfers between devices, local(): lax.all_to_all(left, ('core', 'z', 'yh'), split_axis=0, concat_axis=0, ti...  24.3 us
    all_to_all x1, blocking collectives, local(): right = lax.all_to_all(right, COL, split_axis=0, concat_axis=0, tiled=True)  15.9 us
    all_to_all x1, waiting for transfers between devices, local(): lax.all_to_all(left, ('core', 'z', 'yh'), split_axis=0, concat_axis=0, ti...  12.2 us
    pallas_call x2, Pallas kernels, multiply(): pl.pallas_call(kernel, grid_spec=pltpu.PrefetchScalarGridSpec(num_scalar_...  10.4 us
    pallas_call x1, Pallas kernels, order_left(): pl.pallas_call(kernel, out_shape=jax.ShapeDtypeStruct((2, width, depth),...  4.66 us
    ppermute x1, starting transfers between devices, local(): other = lax.ppermute(right, 'core', [(0, 1), (1, 0)])  4.06 us
  transfers between devices with their start and end apart: 3, of which 2 were waited for; matrix products, arithmetic and copies ran while one was open for 0% of the time, Pallas kernels for 7%

profile of v2, /device:TPU:1, one launch (start us, length us, event | category | flops | bytes accessed | tf_op | source)
XLA Modules:
  0.0 150.9 jit_solution(4820526239902364615)
XLA Ops:
  6.5 0.0 all-gather.2.cloned.1.call-start
  6.5 1.5 %shard_map.64 = bf16[16,2,1280]{2,1,0:T(2,128)(2,1)} custom-call(bf16[1,2,20480]{2,1,0:T(2,128)(2,1)} %in_ref.3), custom_call_target="tpu_custom_call" | custom-call | tf_op jit(solution)/shard_map/pallas_call | solution.py:27
  8.1 15.9 %all_to_all.15.in_ref = bf16[16,2,1280]{2,1,0:T(2,128)(2,1)S(1)} all-to-all(bf16[16,2,1280]{2,1,0:T(2,128)(2,1)} %shard_map.64), channel_id=1, replica_groups=mesh['z'=8,'yh'=4,'core'=2,'yl'=2,'x'=8] {'yl','x'}, dimensions={0} | all-to-all | bytes 163840 | tf_op jit(solution)/shard_map/all_to_all | solution.py:196
  24.0 0.7 shard_map.65
  24.7 0.0 all-gather.2.cloned.1.call-update
  24.8 1.9 %shard_map.66 = bf16[64,2,384]{2,1,0:T(2,128)(2,1)} custom-call(s32[1]{0:T(128)} %bitcast.2.where_ref, s32[1024]{0:T(1024)} %slot_ref.1, s32[1024]{0:T(1024)} %val_ref.1, s32[1024]{0:T(1024)} %cond_ref.1, f32[2048]{0:T(1024)} %upper_ref.1, f32[2048]{0:T(1024)} %lower_ref.1, bf16[1,2,20480]{2,1,0:T(2,128)(2,1)} %in_ref.3), custom_call_target="tpu_custom_call" | custom-call | tf_op jit(solution)/shard_map/pallas_call | solution.py:53
  26.6 24.3 %all-to-all-start.1 = ((bf16[64,2,384]{2,1,0:T(2,128)(2,1)}), bf16[64,2,384]{2,1,0:T(2,128)(2,1)S(1)}, u32[]{:S(2)}, u32[]{:S(2)}) async-start(bf16[64,2,384]{2,1,0:T(2,128)(2,1)} %shard_map.66), calls=%async_computation.1 | async-start | bytes 196608 | tf_op jit(solution)/shard_map/all_to_all | solution.py:200
  50.9 12.2 %all-to-all-done.1.in_ref = bf16[64,2,384]{2,1,0:T(2,128)(2,1)S(1)} async-done(((bf16[64,2,384]{2,1,0:T(2,128)(2,1)}), bf16[64,2,384]{2,1,0:T(2,128)(2,1)S(1)}, u32[]{:S(2)}, u32[]{:S(2)}) %all-to-all-start.1) | async-done | bytes 98336 | tf_op jit(solution)/shard_map/all_to_all | solution.py:200
  63.1 0.3 shard_map.67
  63.4 0.2 broadcast_in_dim.2
  63.7 34.6 %all_to_all.16 = bf16[16,320,128]{2,1,0:T(8,128)(2,1)S(1)} all-to-all(bf16[16,320,128]{2,1,0:T(8,128)(2,1)S(1)} %broadcast_in_dim.2), channel_id=1, replica_groups=mesh['z'=8,'yh'=4,'core'=2,'yl'=2,'x'=8] {'yl','x'}, dimensions={0} | all-to-all | bytes 2621440 | tf_op jit(solution)/shard_map/all_to_all | solution.py:206
  98.3 4.7 %shard_map.68.left_ref = bf16[2,320,2048]{2,1,0:T(8,128)(2,1)S(1)} custom-call(bf16[5120,128]{1,0:T(8,128)(2,1)S(1)} %bitcast.4), custom_call_target="tpu_custom_call" | custom-call | tf_op jit(solution)/shard_map/pallas_call | solution.py:136
  103.0 24.9 %all-gather.2.cloned.1.call-done.right_ref = bf16[1024,1280]{1,0:T(8,128)(2,1)} async-done(((bf16[32,1280]{1,0:T(8,128)(2,1)}), bf16[1024,1280]{1,0:T(8,128)(2,1)}) %all-gather.2.cloned.1.call-update) | async-done | bytes 2621456 | tf_op jit(solution)/shard_map/all_gather | solution.py:202
  127.8 4.1 %collective-permute-start = (bf16[1024,1280]{1,0:T(8,128)(2,1)}, bf16[1024,1280]{1,0:T(8,128)(2,1)S(1)}, u32[]{:S(2)}, u32[]{:S(2)}) collective-permute-start(bf16[1024,1280]{1,0:T(8,128)(2,1)} %all-gather.2.cloned.1.call-done.right_ref), channel_id=1, source_target_pairs={{0,16},{16,0},{1,17},{17,1},{2,18},{18,2},{3,19},{19,3},{4,20},{20... | collective-permute-start | bytes 7864328 | tf_op jit(solution)/shard_map/ppermute | solution.py:210
  131.9 0.0 copy-start
  131.9 1.7 %copy-done = bf16[1024,1280]{1,0:T(8,128)(2,1)S(1)} copy-done((bf16[1024,1280]{1,0:T(8,128)(2,1)S(1)}, bf16[1024,1280]{1,0:T(8,128)(2,1)}, u32[]{:S(2)}) %copy-start) | copy-done | bytes 2621464
  133.6 4.2 %shard_map.69.refs_0_ = f32[2,320,1280]{2,1,0:T(8,128)} custom-call(s32[1]{0:T(128)} %bitcast.half_ref, bf16[2,320,2048]{2,1,0:T(8,128)(2,1)S(1)} %shard_map.68.left_ref, bf16[1024,1280]{1,0:T(8,128)(2,1)S(1)} %copy-done), custom_call_target="tpu_custom_call" | custom-call | flops 1677721600 | bytes 7208960 | tf_op jit(solution)/shard_map/pallas_call | solution.py:159
  137.9 0.0 collective-permute-done.right_ref
  137.9 6.2 %shard_map.70 = f32[2,320,1280]{2,1,0:T(8,128)} custom-call(s32[1]{0:T(128)S(6)} %sub.3.half_ref, bf16[2,320,2048]{2,1,0:T(8,128)(2,1)S(1)} %shard_map.68.left_ref, bf16[1024,1280]{1,0:T(8,128)(2,1)S(1)} %collective-permute-done.right_ref, f32[2,320,1280]{2,1,0:T(8,128)} %shard_map.69.refs_0_), custom_call_target="tpu_custom_call", output_to_operand_aliasing={{}: (3, {})} | custom-call | flops 1677721600 | bytes 7208960 | tf_op jit(solution)/shard_map/pallas_call | solution.py:159
Async XLA Ops:
  6.5 121.3 %all-gather.2.cloned.1.call-start = ((), (), s32[]{:S(2)}) async-start(), calls=%async_computation.3 | async-start | bytes 2703360 | tf_op jit(solution)/shard_map/all_gather | solution.py:202
  26.6 36.5 %all-to-all-start.1 = ((bf16[64,2,384]{2,1,0:T(2,128)(2,1)}), bf16[64,2,384]{2,1,0:T(2,128)(2,1)S(1)}, u32[]{:S(2)}, u32[]{:S(2)}) async-start(bf16[64,2,384]{2,1,0:T(2,128)(2,1)} %shard_map.66), calls=%async_computation.1 | async-start | bytes 196608 | tf_op jit(solution)/shard_map/all_to_all | solution.py:200
  127.8 10.1 %collective-permute-start = (bf16[1024,1280]{1,0:T(8,128)(2,1)}, bf16[1024,1280]{1,0:T(8,128)(2,1)S(1)}, u32[]{:S(2)}, u32[]{:S(2)}) collective-permute-start(bf16[1024,1280]{1,0:T(8,128)(2,1)} %all-gather.2.cloned.1.call-done.right_ref), channel_id=1, source_target_pairs={{0,16},{16,0},{1,17},{17,1},{2,18},{18,2},{3,19},{19,3},{4,20},{20... | collective-permute-start | bytes 7864328 | tf_op jit(solution)/shard_map/ppermute | solution.py:210
  131.9 1.7 %copy-start = (bf16[1024,1280]{1,0:T(8,128)(2,1)S(1)}, bf16[1024,1280]{1,0:T(8,128)(2,1)}, u32[]{:S(2)}) copy-start(bf16[1024,1280]{1,0:T(8,128)(2,1)} %all-gather.2.cloned.1.call-done.right_ref) | copy-start | bytes 7864324
Sparse Core Ops, SparseCore 0:
  24.9 102.9 all-gather.1

commit v3 on v2

--- a/solution.py
+++ b/solution.py
@@ -17,16 +17,18 @@
 WHOLE = pltpu.CompilerParams(vmem_limit_bytes=60 * 1024 * 1024)
 
 
-def split_right(elems, n_col):
+def split_right(elems, n_col, copies):
     width = elems.shape[2] // n_col
 
     def kernel(in_ref, out_ref):
         for block in range(n_col):
-            out_ref[block] = in_ref[0, :, block * width : (block + 1) * width]
-
-    return pl.pallas_call(
-        kernel,
-        out_shape=jax.ShapeDtypeStruct((n_col, 2, width), BF16),
+            part = in_ref[0, :, block * width : (block + 1) * width]
+            for copy in range(copies):
+                out_ref[copy * n_col + block] = part
+
+    return pl.pallas_call(
+        kernel,
+        out_shape=jax.ShapeDtypeStruct((copies * n_col, 2, width), BF16),
         in_specs=[VMEM],
         out_specs=VMEM,
         compiler_params=WHOLE,
@@ -106,25 +108,28 @@
     )(shift, slots)
 
 
-def order_left(slabs, n_row, n_col, width):
+def order_left(slabs, n_row, n_col, n_far, width):
+    group = n_row // n_far
+    near = n_far * n_col
     depth = 2 * n_row * n_col
     half = LANES // 2
     slots = 5 * n_row
 
     def kernel(in_ref, out_ref, real_ref, imag_ref):
         for col in range(n_col):
-            first = pl.ds(col, n_row, stride=2 * n_col)
-            second = pl.ds(n_col + col, n_row, stride=2 * n_col)
-            rows = []
-            for slab in range(5):
-                at = col * slots + slab * n_row
-                rows.append(in_ref[at : at + n_row, :].astype(F32))
-            rows = [(rows[0], rows[2]), (rows[1], rows[3]), (rows[4], pltpu.roll(rows[4], half, 1))]
-            for tile, (re, im) in enumerate(rows):
-                real_ref[tile, first, :] = re
-                real_ref[tile, second, :] = im
-                imag_ref[tile, first, :] = im
-                imag_ref[tile, second, :] = -re
+            for far in range(n_far):
+                first = pl.ds(far * n_col + col, group, stride=2 * near)
+                second = pl.ds(near + far * n_col + col, group, stride=2 * near)
+                rows = []
+                for slab in range(5):
+                    at = col * slots + slab * n_row + far * group
+                    rows.append(in_ref[at : at + group, :].astype(F32))
+                rows = [(rows[0], rows[2]), (rows[1], rows[3]), (rows[4], pltpu.roll(rows[4], half, 1))]
+                for tile, (re, im) in enumerate(rows):
+                    real_ref[tile, first, :] = re
+                    real_ref[tile, second, :] = im
+                    imag_ref[tile, first, :] = im
+                    imag_ref[tile, second, :] = -re
         step = min(256, depth)
         for which, source in enumerate((real_ref, imag_ref)):
             for tile in range(3):
@@ -183,6 +188,8 @@
     full = pair_elems.shape[2]
     n_row = lax.axis_size(ROW)
     n_col = lax.axis_size(COL)
+    n_far = lax.axis_size("yh")
+    n_z = lax.axis_size("z")
     row = lax.axis_index(ROW)
     core = lax.axis_index("core").astype(jnp.int32).reshape(1)
     position = (row * n_col + lax.axis_index(COL)).astype(jnp.int32).reshape(1)
@@ -190,24 +197,26 @@
     span = 3 * LANES
 
     def place_of(block):
-        return block % 2 * (n_row // 2) + block // 2
-
-    right = split_right(pair_elems, n_col)
-    right = lax.all_to_all(right, COL, split_axis=0, concat_axis=0, tiled=True)
+        z, far, side = block // (2 * n_far), block // 2 % n_far, block % 2
+        return (far * 2 + side) * n_z + z
 
     tables = (slot_pair, val_index, cond_index, val_energy, cond_energy)
     left = split_left(pair_elems, tables, position, n_row, span, place_of)
-    left = lax.all_to_all(left, ("core", "z", "yh"), split_axis=0, concat_axis=0, tiled=True)
-
-    right = lax.all_gather(part_rows(right), ("z", "yh"), axis=0, tiled=True)
+    left = lax.all_to_all(left, ("yh", "core", "z"), split_axis=0, concat_axis=0, tiled=True)
+    right = split_right(pair_elems, n_col, n_far)
+    left, right = lax.optimization_barrier((left, right))
+    right = lax.all_to_all(right, ("yh", *COL), split_axis=0, concat_axis=0, tiled=True)
+
     shift = lax.rem(row * width, LANES).astype(jnp.int32).reshape(1)
     left = pack_left(left, shift)
     left = jnp.broadcast_to(left[None], (n_col, *left.shape))
+    right, left = lax.optimization_barrier((right, left))
     left = lax.all_to_all(left, COL, split_axis=0, concat_axis=0, tiled=True)
-    left = order_left(left.reshape(n_col * left.shape[1], LANES), n_row, n_col, width)
+    right = lax.all_gather(part_rows(right), "z", axis=0, tiled=True)
     right, left = lax.optimization_barrier((right, left))
 
     other = lax.ppermute(right, "core", [(0, 1), (1, 0)])
+    left = order_left(left.reshape(n_col * left.shape[1], LANES), n_row, n_col, n_far, width)
     total = multiply(core, left, right)
     return multiply(1 - core, left, other, total)
 

time: 151 us -> 135 us (0.89)
  blocking collectives: 50.6 us -> 34.6 us
  waiting for transfers between devices: 37.1 us -> 26.1 us
  starting transfers between devices: 28.3 us -> 39 us
  local copies, waits for them, and re-layouts: 1.98 us -> 0.25 us
    all_gather x1, waiting for transfers between devices: 24.9 us -> 2.48 us  [local(): right = lax.all_gather(part_rows(right), 'z', axis=0, tiled=True)]
    all_to_all x1 -> x0, blocking collectives: 15.9 us -> none  [local(): right = lax.all_to_all(right, COL, split_axis=0, concat_axis=0, tiled=True)]
    all_to_all x1 -> x2, waiting for transfers between devices: 12.2 us -> 23.6 us  [the longest x1 13.3 us: local(): lax.all_to_all(right, ('yh', *COL), split_axis=0, concat_axis=0, tiled=True)]
    all_to_all x1 -> x2, starting transfers between devices: 24.3 us -> 33.2 us  [the longest x1 24.5 us: local(): lax.all_to_all(left, ('yh', 'core', 'z'), split_axis=0, concat_axis=0, ti...]
    unnamed x2, local copies, waits for them, and re-layouts: 1.73 us -> 0.01 us
    ppermute x1, starting transfers between devices: 4.06 us -> 5.7 us  [local(): other = lax.ppermute(right, 'core', [(0, 1), (1, 0)])]
  transfers between devices with their start and end apart: 3 -> 4, of which waited for: 2 -> 3; matrix products, arithmetic and copies ran while one was open for 0% -> 0% of each run, Pallas kernels for 7% -> 9%
where the time goes in v3:
time: 135 us; the launch traced here: 134 us
  starting transfers between devices  39 us (29%)
  blocking collectives  34.6 us (26%)
  waiting for transfers between devices  26.1 us (19%)
  Pallas kernels  20.7 us (15%)
  between operations  13.5 us (10%)
    all_to_all x1, blocking collectives, local(): left = lax.all_to_all(left, COL, split_axis=0, concat_axis=0, tiled=True)  34.6 us
    all_to_all x1, starting transfers between devices, local(): lax.all_to_all(left, ('yh', 'core', 'z'), split_axis=0, concat_axis=0, ti...  24.5 us
    all_to_all x1, waiting for transfers between devices, local(): lax.all_to_all(right, ('yh', *COL), split_axis=0, concat_axis=0, tiled=True)  13.3 us
    pallas_call x2, Pallas kernels, multiply(): pl.pallas_call(kernel, grid_spec=pltpu.PrefetchScalarGridSpec(num_scalar_...  10.5 us
    all_to_all x1, waiting for transfers between devices, local(): lax.all_to_all(left, ('yh', 'core', 'z'), split_axis=0, concat_axis=0, ti...  10.3 us
    all_to_all x1, starting transfers between devices, local(): lax.all_to_all(right, ('yh', *COL), split_axis=0, concat_axis=0, tiled=True)  8.78 us
    ppermute x1, starting transfers between devices, local(): other = lax.ppermute(right, 'core', [(0, 1), (1, 0)])  5.7 us
    pallas_call x1, Pallas kernels, order_left(): pl.pallas_call(kernel, out_shape=jax.ShapeDtypeStruct((2, width, depth),...  5.23 us
  transfers between devices with their start and end apart: 4, of which 3 were waited for; matrix products, arithmetic and copies ran while one was open for 0% of the time, Pallas kernels for 9%

profile of v3, /device:TPU:1, one launch (start us, length us, event | category | flops | bytes accessed | tf_op | source)
XLA Modules:
  0.0 134.1 jit_solution(7181368731353064692)
XLA Ops:
  6.5 1.8 %shard_map.64 = bf16[64,2,384]{2,1,0:T(2,128)(2,1)} custom-call(s32[1]{0:T(128)} %bitcast.1.where_ref, s32[1024]{0:T(1024)} %slot_ref.1, s32[1024]{0:T(1024)} %val_ref.1, s32[1024]{0:T(1024)} %cond_ref.1, f32[2048]{0:T(1024)} %upper_ref.1, f32[2048]{0:T(1024)} %lower_ref.1, bf16[1,2,20480]{2,1,0:T(2,128)(2,1)} %in_ref.3), custom_call_target="tpu_custom_call" | custom-call | tf_op jit(solution)/shard_map/pallas_call | solution.py:55
  8.4 24.5 %all-to-all-start = ((bf16[64,2,384]{2,1,0:T(2,128)(2,1)}), bf16[64,2,384]{2,1,0:T(2,128)(2,1)S(1)}, u32[]{:S(2)}, u32[]{:S(2)}) async-start(bf16[64,2,384]{2,1,0:T(2,128)(2,1)} %shard_map.64), calls=%async_computation | async-start | bytes 196608 | tf_op jit(solution)/shard_map/all_to_all | solution.py:205
  32.9 1.6 %shard_map.65 = bf16[64,2,1280]{2,1,0:T(2,128)(2,1)} custom-call(bf16[1,2,20480]{2,1,0:T(2,128)(2,1)} %in_ref.3), custom_call_target="tpu_custom_call" | custom-call | tf_op jit(solution)/shard_map/pallas_call | solution.py:29
  34.5 10.3 %all-to-all-done.in_ref = bf16[64,2,384]{2,1,0:T(2,128)(2,1)S(1)} async-done(((bf16[64,2,384]{2,1,0:T(2,128)(2,1)}), bf16[64,2,384]{2,1,0:T(2,128)(2,1)S(1)}, u32[]{:S(2)}, u32[]{:S(2)}) %all-to-all-start) | async-done | bytes 98336 | tf_op jit(solution)/shard_map/all_to_all | solution.py:205
  44.8 8.8 %all-to-all-start.1 = ((bf16[64,2,1280]{2,1,0:T(2,128)(2,1)}), bf16[64,2,1280]{2,1,0:T(2,128)(2,1)S(1)}, u32[]{:S(2)}, u32[]{:S(2)}) async-start(bf16[64,2,1280]{2,1,0:T(2,128)(2,1)} %shard_map.65), calls=%async_computation.1 | async-start | bytes 655360 | tf_op jit(solution)/shard_map/all_to_all | solution.py:208
  53.6 0.0 all-gather.2.cloned.1.call-start
  53.7 0.3 shard_map.66
  53.9 13.3 %all-to-all-done.1.in_ref = bf16[64,2,1280]{2,1,0:T(2,128)(2,1)S(1)} async-done(((bf16[64,2,1280]{2,1,0:T(2,128)(2,1)}), bf16[64,2,1280]{2,1,0:T(2,128)(2,1)S(1)}, u32[]{:S(2)}, u32[]{:S(2)}) %all-to-all-start.1) | async-done | bytes 327712 | tf_op jit(solution)/shard_map/all_to_all | solution.py:208
  67.2 0.2 broadcast_in_dim.2
  67.5 1.2 shard_map.67
  68.7 0.0 all-gather.2.cloned.1.call-update
  68.7 34.6 %all_to_all.15 = bf16[16,320,128]{2,1,0:T(8,128)(2,1)S(1)} all-to-all(bf16[16,320,128]{2,1,0:T(8,128)(2,1)S(1)} %broadcast_in_dim.2), channel_id=1, replica_groups=mesh['z'=8,'yh'=4,'core'=2,'yl'=2,'x'=8] {'yl','x'}, dimensions={0} | all-to-all | bytes 2621440 | tf_op jit(solution)/shard_map/all_to_all | solution.py:214
  103.4 2.5 %all-gather.2.cloned.1.call-done.right_ref = bf16[1024,1280]{1,0:T(8,128)(2,1)} async-done(((bf16[128,1280]{1,0:T(8,128)(2,1)}), bf16[1024,1280]{1,0:T(8,128)(2,1)}) %all-gather.2.cloned.1.call-update) | async-done | bytes 2621456 | tf_op jit(solution)/shard_map/all_gather | solution.py:215
  105.8 0.0 copy-start
  105.8 5.7 %collective-permute-start = (bf16[1024,1280]{1,0:T(8,128)(2,1)}, bf16[1024,1280]{1,0:T(8,128)(2,1)S(1)}, u32[]{:S(2)}, u32[]{:S(2)}) collective-permute-start(bf16[1024,1280]{1,0:T(8,128)(2,1)} %all-gather.2.cloned.1.call-done.right_ref), channel_id=1, source_target_pairs={{0,16},{16,0},{1,17},{17,1},{2,18},{18,2},{3,19},{19,3},{4,20},{20... | collective-permute-start | bytes 7864328 | tf_op jit(solution)/shard_map/ppermute | solution.py:218
  111.5 5.2 %shard_map.68.left_ref = bf16[2,320,2048]{2,1,0:T(8,128)(2,1)S(1)} custom-call(bf16[5120,128]{1,0:T(8,128)(2,1)S(1)} %bitcast.4), custom_call_target="tpu_custom_call" | custom-call | tf_op jit(solution)/shard_map/pallas_call | solution.py:141
  116.8 0.0 copy-done
  116.8 4.3 %shard_map.69.refs_0_ = f32[2,320,1280]{2,1,0:T(8,128)} custom-call(s32[1]{0:T(128)} %bitcast.half_ref, bf16[2,320,2048]{2,1,0:T(8,128)(2,1)S(1)} %shard_map.68.left_ref, bf16[1024,1280]{1,0:T(8,128)(2,1)S(1)} %copy-done), custom_call_target="tpu_custom_call" | custom-call | flops 1677721600 | bytes 7208960 | tf_op jit(solution)/shard_map/pallas_call | solution.py:164
  121.1 0.0 collective-permute-done.right_ref
  121.1 6.2 %shard_map.70 = f32[2,320,1280]{2,1,0:T(8,128)} custom-call(s32[1]{0:T(128)S(6)} %sub.3.half_ref, bf16[2,320,2048]{2,1,0:T(8,128)(2,1)S(1)} %shard_map.68.left_ref, bf16[1024,1280]{1,0:T(8,128)(2,1)S(1)} %collective-permute-done.right_ref, f32[2,320,1280]{2,1,0:T(8,128)} %shard_map.69.refs_0_), custom_call_target="tpu_custom_call", output_to_operand_aliasing={{}: (3, {})} | custom-call | flops 1677721600 | bytes 7208960 | tf_op jit(solution)/shard_map/pallas_call | solution.py:164
Async XLA Ops:
  8.4 36.4 %all-to-all-start = ((bf16[64,2,384]{2,1,0:T(2,128)(2,1)}), bf16[64,2,384]{2,1,0:T(2,128)(2,1)S(1)}, u32[]{:S(2)}, u32[]{:S(2)}) async-start(bf16[64,2,384]{2,1,0:T(2,128)(2,1)} %shard_map.64), calls=%async_computation | async-start | bytes 196608 | tf_op jit(solution)/shard_map/all_to_all | solution.py:205
  44.8 22.4 %all-to-all-start.1 = ((bf16[64,2,1280]{2,1,0:T(2,128)(2,1)}), bf16[64,2,1280]{2,1,0:T(2,128)(2,1)S(1)}, u32[]{:S(2)}, u32[]{:S(2)}) async-start(bf16[64,2,1280]{2,1,0:T(2,128)(2,1)} %shard_map.65), calls=%async_computation.1 | async-start | bytes 655360 | tf_op jit(solution)/shard_map/all_to_all | solution.py:208
  53.6 52.2 %all-gather.2.cloned.1.call-start = ((), (), s32[]{:S(2)}) async-start(), calls=%async_computation.3 | async-start | bytes 2949120 | tf_op jit(solution)/shard_map/all_gather | solution.py:215
  105.8 10.9 %copy-start = (bf16[1024,1280]{1,0:T(8,128)(2,1)S(1)}, bf16[1024,1280]{1,0:T(8,128)(2,1)}, u32[]{:S(2)}) copy-start(bf16[1024,1280]{1,0:T(8,128)(2,1)} %all-gather.2.cloned.1.call-done.right_ref) | copy-start | bytes 7864324
  105.8 15.2 %collective-permute-start = (bf16[1024,1280]{1,0:T(8,128)(2,1)}, bf16[1024,1280]{1,0:T(8,128)(2,1)S(1)}, u32[]{:S(2)}, u32[]{:S(2)}) collective-permute-start(bf16[1024,1280]{1,0:T(8,128)(2,1)} %all-gather.2.cloned.1.call-done.right_ref), channel_id=1, source_target_pairs={{0,16},{16,0},{1,17},{17,1},{2,18},{18,2},{3,19},{19,3},{4,20},{20... | collective-permute-start | bytes 7864328 | tf_op jit(solution)/shard_map/ppermute | solution.py:218
Sparse Core Ops, SparseCore 0:
  68.8 36.9 all-gather.1

commit v4 on v3

--- a/solution.py
+++ b/solution.py
@@ -114,36 +114,37 @@
     depth = 2 * n_row * n_col
     half = LANES // 2
     slots = 5 * n_row
-
-    def kernel(in_ref, out_ref, real_ref, imag_ref):
+    step = 2 * near
+
+    def kernel(in_ref, out_ref, rows_ref):
         for col in range(n_col):
             for far in range(n_far):
-                first = pl.ds(far * n_col + col, group, stride=2 * near)
-                second = pl.ds(near + far * n_col + col, group, stride=2 * near)
+                first = pl.ds(far * n_col + col, group, stride=step)
+                second = pl.ds(near + far * n_col + col, group, stride=step)
                 rows = []
                 for slab in range(5):
                     at = col * slots + slab * n_row + far * group
                     rows.append(in_ref[at : at + group, :].astype(F32))
                 rows = [(rows[0], rows[2]), (rows[1], rows[3]), (rows[4], pltpu.roll(rows[4], half, 1))]
                 for tile, (re, im) in enumerate(rows):
-                    real_ref[tile, first, :] = re
-                    real_ref[tile, second, :] = im
-                    imag_ref[tile, first, :] = im
-                    imag_ref[tile, second, :] = -re
-        step = min(256, depth)
-        for which, source in enumerate((real_ref, imag_ref)):
-            for tile in range(3):
-                keep = min(LANES, width - tile * LANES)
-                for at in range(0, depth, step):
-                    turned = source[tile, at : at + step, :].T.astype(BF16)
-                    out_ref[which, tile * LANES : tile * LANES + keep, at : at + step] = turned[:keep]
+                    rows_ref[tile, first, :] = re
+                    rows_ref[tile, second, :] = im
+        sign = jnp.where(lax.broadcasted_iota(jnp.int32, (LANES, step), 1) < near, 1.0, -1.0)
+        for tile in range(3):
+            keep = min(LANES, width - tile * LANES)
+            here = slice(tile * LANES, tile * LANES + keep)
+            for at in range(0, depth, step):
+                turned = rows_ref[tile, at : at + step, :].T
+                out_ref[0, here, at : at + step] = turned[:keep].astype(BF16)
+                turned = pltpu.roll(turned, near, 1) * sign
+                out_ref[1, here, at : at + step] = turned[:keep].astype(BF16)
 
     return pl.pallas_call(
         kernel,
         out_shape=jax.ShapeDtypeStruct((2, width, depth), BF16),
         in_specs=[VMEM],
         out_specs=VMEM,
-        scratch_shapes=[pltpu.VMEM((3, depth, LANES), F32), pltpu.VMEM((3, depth, LANES), F32)],
+        scratch_shapes=[pltpu.VMEM((3, depth, LANES), F32)],
         compiler_params=LIMIT,
     )(slabs)
 
@@ -155,26 +156,22 @@
 
     def kernel(half_ref, left_ref, right_ref, *refs):
         out_ref = refs[-1]
+        now = pl.ds(pl.multiple_of(pl.program_id(0) * step, step), step)
         for which in range(2):
-            product = jnp.dot(left_ref[which], right_ref[...], preferred_element_type=F32)
-            out_ref[which] = product if total is None else refs[0][which] + product
-
-    out_spec = pl.BlockSpec((2, width, step), lambda j, half_ref: (0, 0, j))
+            product = jnp.dot(left_ref[which], right_ref[:, now], preferred_element_type=F32)
+            out_ref[which] = product if total is None else refs[0][which, :, now] + product
+
     extra = [] if total is None else [total]
     return pl.pallas_call(
         kernel,
         grid_spec=pltpu.PrefetchScalarGridSpec(
             num_scalar_prefetch=1,
             grid=(columns // step,),
-            in_specs=[
-                pl.BlockSpec((2, width, depth), lambda j, half_ref: (0, 0, half_ref[0])),
-                pl.BlockSpec((depth, step), lambda j, half_ref: (0, j)),
-            ]
-            + [out_spec] * len(extra),
-            out_specs=out_spec,
+            in_specs=[pl.BlockSpec((2, width, depth), lambda j, half_ref: (0, 0, half_ref[0])), VMEM]
+            + [VMEM] * len(extra),
+            out_specs=pl.BlockSpec((2, width, step), lambda j, half_ref: (0, 0, j)),
         ),
         out_shape=jax.ShapeDtypeStruct((2, width, columns), F32),
-        input_output_aliases={3: 0} if extra else {},
         compiler_params=LIMIT,
         cost_estimate=pl.CostEstimate(
             flops=4 * width * depth * columns,
@@ -213,10 +210,10 @@
     right, left = lax.optimization_barrier((right, left))
     left = lax.all_to_all(left, COL, split_axis=0, concat_axis=0, tiled=True)
     right = lax.all_gather(part_rows(right), "z", axis=0, tiled=True)
+    left = order_left(left.reshape(n_col * left.shape[1], LANES), n_row, n_col, n_far, width)
     right, left = lax.optimization_barrier((right, left))
 
     other = lax.ppermute(right, "core", [(0, 1), (1, 0)])
-    left = order_left(left.reshape(n_col * left.shape[1], LANES), n_row, n_col, n_far, width)
     total = multiply(core, left, right)
     return multiply(1 - core, left, other, total)
 

time: 135 us -> 131 us (0.970)
  waiting for transfers between devices: 26.1 us -> 23.6 us
  Pallas kernels: 20.7 us -> 18.3 us
  local copies, waits for them, and re-layouts: 0.25 us -> 1.98 us
    all_gather x1, waiting for transfers between devices: 2.48 us -> 0.02 us  [local(): right = lax.all_gather(part_rows(right), 'z', axis=0, tiled=True)]
    pallas_call x1, Pallas kernels: 5.23 us -> 2.91 us  [order_left(): pl.pallas_call(kernel, out_shape=jax.ShapeDtypeStruct((2, width, depth),...]
    unnamed x2, local copies, waits for them, and re-layouts: 0.01 us -> 1.73 us
  transfers between devices with their start and end apart: 4 -> 4, of which waited for: 3 -> 2; matrix products, arithmetic and copies ran while one was open for 0% -> 0% of each run, Pallas kernels for 9% -> 7%
where the time goes in v4:
time: 131 us
  starting transfers between devices  38.7 us (30%)
  blocking collectives  34.6 us (26%)
  waiting for transfers between devices  23.6 us (18%)
  Pallas kernels  18.3 us (14%)
  between operations  13.5 us (10%)
  local copies, waits for them, and re-layouts  1.98 us (2%)
    all_to_all x1, blocking collectives, local(): left = lax.all_to_all(left, COL, split_axis=0, concat_axis=0, tiled=True)  34.6 us
    all_to_all x1, starting transfers between devices, local(): lax.all_to_all(left, ('yh', 'core', 'z'), split_axis=0, concat_axis=0, ti...  24.5 us
    all_to_all x1, waiting for transfers between devices, local(): lax.all_to_all(right, ('yh', *COL), split_axis=0, concat_axis=0, tiled=True)  13.3 us
    pallas_call x2, Pallas kernels, multiply(): pl.pallas_call(kernel, grid_spec=pltpu.PrefetchScalarGridSpec(num_scalar_...  10.4 us
    all_to_all x1, waiting for transfers between devices, local(): lax.all_to_all(left, ('yh', 'core', 'z'), split_axis=0, concat_axis=0, ti...  10.3 us
    all_to_all x1, starting transfers between devices, local(): lax.all_to_all(right, ('yh', *COL), split_axis=0, concat_axis=0, tiled=True)  8.78 us
    ppermute x1, starting transfers between devices, local(): other = lax.ppermute(right, 'core', [(0, 1), (1, 0)])  5.43 us
    pallas_call x1, Pallas kernels, order_left(): pl.pallas_call(kernel, out_shape=jax.ShapeDtypeStruct((2, width, depth),...  2.91 us
  transfers between devices with their start and end apart: 4, of which 2 were waited for; matrix products, arithmetic and copies ran while one was open for 0% of the time, Pallas kernels for 7%

profile of v4, /device:TPU:1, one launch (start us, length us, event | category | flops | bytes accessed | tf_op | source)
XLA Modules:
  0.0 130.7 jit_solution(530090161527093874)
XLA Ops:
  6.5 1.8 %shard_map.64 = bf16[64,2,384]{2,1,0:T(2,128)(2,1)} custom-call(s32[1]{0:T(128)} %bitcast.1.where_ref, s32[1024]{0:T(1024)} %slot_ref.1, s32[1024]{0:T(1024)} %val_ref.1, s32[1024]{0:T(1024)} %cond_ref.1, f32[2048]{0:T(1024)} %upper_ref.1, f32[2048]{0:T(1024)} %lower_ref.1, bf16[1,2,20480]{2,1,0:T(2,128)(2,1)} %in_ref.3), custom_call_target="tpu_custom_call" | custom-call | tf_op jit(solution)/shard_map/pallas_call | solution.py:55
  8.4 24.5 %all-to-all-start = ((bf16[64,2,384]{2,1,0:T(2,128)(2,1)}), bf16[64,2,384]{2,1,0:T(2,128)(2,1)S(1)}, u32[]{:S(2)}, u32[]{:S(2)}) async-start(bf16[64,2,384]{2,1,0:T(2,128)(2,1)} %shard_map.64), calls=%async_computation | async-start | bytes 196608 | tf_op jit(solution)/shard_map/all_to_all | solution.py:202
  32.9 1.6 %shard_map.65 = bf16[64,2,1280]{2,1,0:T(2,128)(2,1)} custom-call(bf16[1,2,20480]{2,1,0:T(2,128)(2,1)} %in_ref.3), custom_call_target="tpu_custom_call" | custom-call | tf_op jit(solution)/shard_map/pallas_call | solution.py:29
  34.5 10.3 %all-to-all-done.in_ref = bf16[64,2,384]{2,1,0:T(2,128)(2,1)S(1)} async-done(((bf16[64,2,384]{2,1,0:T(2,128)(2,1)}), bf16[64,2,384]{2,1,0:T(2,128)(2,1)S(1)}, u32[]{:S(2)}, u32[]{:S(2)}) %all-to-all-start) | async-done | bytes 98336 | tf_op jit(solution)/shard_map/all_to_all | solution.py:202
  44.8 8.8 %all-to-all-start.1 = ((bf16[64,2,1280]{2,1,0:T(2,128)(2,1)}), bf16[64,2,1280]{2,1,0:T(2,128)(2,1)S(1)}, u32[]{:S(2)}, u32[]{:S(2)}) async-start(bf16[64,2,1280]{2,1,0:T(2,128)(2,1)} %shard_map.65), calls=%async_computation.1 | async-start | bytes 655360 | tf_op jit(solution)/shard_map/all_to_all | solution.py:205
  53.6 0.0 all-gather.2.cloned.1.call-start
  53.7 0.3 shard_map.66
  53.9 13.3 %all-to-all-done.1.in_ref = bf16[64,2,1280]{2,1,0:T(2,128)(2,1)S(1)} async-done(((bf16[64,2,1280]{2,1,0:T(2,128)(2,1)}), bf16[64,2,1280]{2,1,0:T(2,128)(2,1)S(1)}, u32[]{:S(2)}, u32[]{:S(2)}) %all-to-all-start.1) | async-done | bytes 327712 | tf_op jit(solution)/shard_map/all_to_all | solution.py:205
  67.2 0.2 broadcast_in_dim.2
  67.5 1.2 shard_map.67
  68.7 0.0 all-gather.2.cloned.1.call-update
  68.7 34.6 %all_to_all.15 = bf16[16,320,128]{2,1,0:T(8,128)(2,1)S(1)} all-to-all(bf16[16,320,128]{2,1,0:T(8,128)(2,1)S(1)} %broadcast_in_dim.2), channel_id=1, replica_groups=mesh['z'=8,'yh'=4,'core'=2,'yl'=2,'x'=8] {'yl','x'}, dimensions={0} | all-to-all | bytes 2621440 | tf_op jit(solution)/shard_map/all_to_all | solution.py:211
  103.4 2.9 %shard_map.68.left_ref = bf16[2,320,2048]{2,1,0:T(8,128)(2,1)S(1)} custom-call(bf16[5120,128]{1,0:T(8,128)(2,1)S(1)} %bitcast.4), custom_call_target="tpu_custom_call" | custom-call | tf_op jit(solution)/shard_map/pallas_call | solution.py:142
  106.3 0.0 all-gather.2.cloned.1.call-done.right_ref
  106.3 5.4 %collective-permute-start = (bf16[1024,1280]{1,0:T(8,128)(2,1)}, bf16[1024,1280]{1,0:T(8,128)(2,1)S(1)}, u32[]{:S(2)}, u32[]{:S(2)}) collective-permute-start(bf16[1024,1280]{1,0:T(8,128)(2,1)} %all-gather.2.cloned.1.call-done.right_ref), channel_id=1, source_target_pairs={{0,16},{16,0},{1,17},{17,1},{2,18},{18,2},{3,19},{19,3},{4,20},{20... | collective-permute-start | bytes 7864328 | tf_op jit(solution)/shard_map/ppermute | solution.py:216
  111.7 0.0 copy-start
  111.8 1.7 %copy-done = bf16[1024,1280]{1,0:T(8,128)(2,1)S(1)} copy-done((bf16[1024,1280]{1,0:T(8,128)(2,1)S(1)}, bf16[1024,1280]{1,0:T(8,128)(2,1)}, u32[]{:S(2)}) %copy-start) | copy-done | bytes 2621464
  113.5 4.4 %shard_map.69.refs_0_ = f32[2,320,1280]{2,1,0:T(8,128)} custom-call(s32[1]{0:T(128)} %bitcast.half_ref, bf16[2,320,2048]{2,1,0:T(8,128)(2,1)S(1)} %shard_map.68.left_ref, bf16[1024,1280]{1,0:T(8,128)(2,1)S(1)} %copy-done), custom_call_target="tpu_custom_call" | custom-call | flops 1677721600 | bytes 7208960 | tf_op jit(solution)/shard_map/pallas_call | solution.py:165
  117.8 0.0 collective-permute-done.right_ref
  117.8 6.0 %shard_map.70 = f32[2,320,1280]{2,1,0:T(8,128)} custom-call(s32[1]{0:T(128)S(6)} %sub.3.half_ref, bf16[2,320,2048]{2,1,0:T(8,128)(2,1)S(1)} %shard_map.68.left_ref, bf16[1024,1280]{1,0:T(8,128)(2,1)S(1)} %collective-permute-done.right_ref, f32[2,320,1280]{2,1,0:T(8,128)} %shard_map.69.refs_0_), custom_call_target="tpu_custom_call" | custom-call | flops 1677721600 | bytes 7208960 | tf_op jit(solution)/shard_map/pallas_call | solution.py:165
Async XLA Ops:
  8.4 36.4 %all-to-all-start = ((bf16[64,2,384]{2,1,0:T(2,128)(2,1)}), bf16[64,2,384]{2,1,0:T(2,128)(2,1)S(1)}, u32[]{:S(2)}, u32[]{:S(2)}) async-start(bf16[64,2,384]{2,1,0:T(2,128)(2,1)} %shard_map.64), calls=%async_computation | async-start | bytes 196608 | tf_op jit(solution)/shard_map/all_to_all | solution.py:202
  44.8 22.4 %all-to-all-start.1 = ((bf16[64,2,1280]{2,1,0:T(2,128)(2,1)}), bf16[64,2,1280]{2,1,0:T(2,128)(2,1)S(1)}, u32[]{:S(2)}, u32[]{:S(2)}) async-start(bf16[64,2,1280]{2,1,0:T(2,128)(2,1)} %shard_map.65), calls=%async_computation.1 | async-start | bytes 655360 | tf_op jit(solution)/shard_map/all_to_all | solution.py:205
  53.6 52.7 %all-gather.2.cloned.1.call-start = ((), (), s32[]{:S(2)}) async-start(), calls=%async_computation.3 | async-start | bytes 2949120 | tf_op jit(solution)/shard_map/all_gather | solution.py:212
  106.3 11.5 %collective-permute-start = (bf16[1024,1280]{1,0:T(8,128)(2,1)}, bf16[1024,1280]{1,0:T(8,128)(2,1)S(1)}, u32[]{:S(2)}, u32[]{:S(2)}) collective-permute-start(bf16[1024,1280]{1,0:T(8,128)(2,1)} %all-gather.2.cloned.1.call-done.right_ref), channel_id=1, source_target_pairs={{0,16},{16,0},{1,17},{17,1},{2,18},{18,2},{3,19},{19,3},{4,20},{20... | collective-permute-start | bytes 7864328 | tf_op jit(solution)/shard_map/ppermute | solution.py:216
  111.7 1.7 %copy-start = (bf16[1024,1280]{1,0:T(8,128)(2,1)S(1)}, bf16[1024,1280]{1,0:T(8,128)(2,1)}, u32[]{:S(2)}) copy-start(bf16[1024,1280]{1,0:T(8,128)(2,1)} %all-gather.2.cloned.1.call-done.right_ref) | copy-start | bytes 7864324
Sparse Core Ops, SparseCore 0:
  68.8 36.9 all-gather.1

commit v5 on v4

--- a/solution.py
+++ b/solution.py
@@ -14,6 +14,7 @@
 VMEM = pl.BlockSpec(memory_space=pltpu.VMEM)
 SMEM = pl.BlockSpec(memory_space=pltpu.SMEM)
 LIMIT = pltpu.CompilerParams(vmem_limit_bytes=48 * 1024 * 1024)
+SMALL = pltpu.CompilerParams(vmem_limit_bytes=32 * 1024 * 1024)
 WHOLE = pltpu.CompilerParams(vmem_limit_bytes=60 * 1024 * 1024)
 
 
@@ -155,11 +156,13 @@
     step = 256
 
     def kernel(half_ref, left_ref, right_ref, *refs):
-        out_ref = refs[-1]
         now = pl.ds(pl.multiple_of(pl.program_id(0) * step, step), step)
         for which in range(2):
-            product = jnp.dot(left_ref[which], right_ref[:, now], preferred_element_type=F32)
-            out_ref[which] = product if total is None else refs[0][which, :, now] + product
+            product = jnp.dot(left_ref[which], right_ref[:, now] if extra else right_ref[...], preferred_element_type=F32)
+            if total is None:
+                refs[0][which, :, now] = product
+            else:
+                refs[1][which] = refs[0][which, :, now] + product
 
     extra = [] if total is None else [total]
     return pl.pallas_call(
@@ -167,12 +170,12 @@
         grid_spec=pltpu.PrefetchScalarGridSpec(
             num_scalar_prefetch=1,
             grid=(columns // step,),
-            in_specs=[pl.BlockSpec((2, width, depth), lambda j, half_ref: (0, 0, half_ref[0])), VMEM]
+            in_specs=[pl.BlockSpec((2, width, depth), lambda j, half_ref: (0, 0, half_ref[0])), VMEM if extra else pl.BlockSpec((depth, step), lambda j, half_ref: (0, j))]
             + [VMEM] * len(extra),
-            out_specs=pl.BlockSpec((2, width, step), lambda j, half_ref: (0, 0, j)),
+            out_specs=pl.BlockSpec((2, width, step), lambda j, half_ref: (0, 0, j)) if extra else VMEM,
         ),
         out_shape=jax.ShapeDtypeStruct((2, width, columns), F32),
-        compiler_params=LIMIT,
+        compiler_params=SMALL,
         cost_estimate=pl.CostEstimate(
             flops=4 * width * depth * columns,
             bytes_accessed=2 * depth * (2 * width + columns) + 8 * width * columns,

time: 131 us -> 128 us (0.977)
  Pallas kernels: 18.3 us -> 14.9 us
    pallas_call x2, Pallas kernels: 10.4 us -> 7.02 us  [multiply(): pl.pallas_call(kernel, grid_spec=pltpu.PrefetchScalarGridSpec(num_scalar_...]
  transfers between devices with their start and end apart: 4 -> 4, of which waited for: 2 -> 3; matrix products, arithmetic and copies ran while one was open for 0% -> 0% of each run, Pallas kernels for 7% -> 6%
where the time goes in v5:
time: 128 us; the launch traced here: 127 us
  starting transfers between devices  38.7 us (30%)
  blocking collectives  34.6 us (27%)
  waiting for transfers between devices  23.7 us (19%)
  Pallas kernels  14.9 us (12%)
  between operations  13.5 us (11%)
  local copies, waits for them, and re-layouts  1.98 us (2%)
    all_to_all x1, blocking collectives, local(): left = lax.all_to_all(left, COL, split_axis=0, concat_axis=0, tiled=True)  34.6 us
    all_to_all x1, starting transfers between devices, local(): lax.all_to_all(left, ('yh', 'core', 'z'), split_axis=0, concat_axis=0, ti...  24.5 us
    all_to_all x1, waiting for transfers between devices, local(): lax.all_to_all(right, ('yh', *COL), split_axis=0, concat_axis=0, tiled=True)  13.3 us
    all_to_all x1, waiting for transfers between devices, local(): lax.all_to_all(left, ('yh', 'core', 'z'), split_axis=0, concat_axis=0, ti...  10.3 us
    all_to_all x1, starting transfers between devices, local(): lax.all_to_all(right, ('yh', *COL), split_axis=0, concat_axis=0, tiled=True)  8.78 us
    pallas_call x2, Pallas kernels, multiply(): pl.pallas_call(kernel, grid_spec=pltpu.PrefetchScalarGridSpec(num_scalar_...  7.02 us
    ppermute x1, starting transfers between devices, local(): other = lax.ppermute(right, 'core', [(0, 1), (1, 0)])  5.43 us
    pallas_call x1, Pallas kernels, order_left(): pl.pallas_call(kernel, out_shape=jax.ShapeDtypeStruct((2, width, depth),...  2.91 us
  transfers between devices with their start and end apart: 4, of which 3 were waited for; matrix products, arithmetic and copies ran while one was open for 0% of the time, Pallas kernels for 6%

profile of v5, /device:TPU:1, one launch (start us, length us, event | category | flops | bytes accessed | tf_op | source)
XLA Modules:
  0.0 127.4 jit_solution(15758907252117304797)
XLA Ops:
  6.5 1.8 %shard_map.64 = bf16[64,2,384]{2,1,0:T(2,128)(2,1)} custom-call(s32[1]{0:T(128)} %bitcast.1.where_ref, s32[1024]{0:T(1024)} %slot_ref.1, s32[1024]{0:T(1024)} %val_ref.1, s32[1024]{0:T(1024)} %cond_ref.1, f32[2048]{0:T(1024)} %upper_ref.1, f32[2048]{0:T(1024)} %lower_ref.1, bf16[1,2,20480]{2,1,0:T(2,128)(2,1)} %in_ref.3), custom_call_target="tpu_custom_call" | custom-call | tf_op jit(solution)/shard_map/pallas_call | solution.py:56
  8.4 24.5 %all-to-all-start = ((bf16[64,2,384]{2,1,0:T(2,128)(2,1)}), bf16[64,2,384]{2,1,0:T(2,128)(2,1)S(1)}, u32[]{:S(2)}, u32[]{:S(2)}) async-start(bf16[64,2,384]{2,1,0:T(2,128)(2,1)} %shard_map.64), calls=%async_computation | async-start | bytes 196608 | tf_op jit(solution)/shard_map/all_to_all | solution.py:205
  32.9 1.6 %shard_map.65 = bf16[64,2,1280]{2,1,0:T(2,128)(2,1)} custom-call(bf16[1,2,20480]{2,1,0:T(2,128)(2,1)} %in_ref.3), custom_call_target="tpu_custom_call" | custom-call | tf_op jit(solution)/shard_map/pallas_call | solution.py:30
  34.5 10.3 %all-to-all-done.in_ref = bf16[64,2,384]{2,1,0:T(2,128)(2,1)S(1)} async-done(((bf16[64,2,384]{2,1,0:T(2,128)(2,1)}), bf16[64,2,384]{2,1,0:T(2,128)(2,1)S(1)}, u32[]{:S(2)}, u32[]{:S(2)}) %all-to-all-start) | async-done | bytes 98336 | tf_op jit(solution)/shard_map/all_to_all | solution.py:205
  44.8 8.8 %all-to-all-start.1 = ((bf16[64,2,1280]{2,1,0:T(2,128)(2,1)}), bf16[64,2,1280]{2,1,0:T(2,128)(2,1)S(1)}, u32[]{:S(2)}, u32[]{:S(2)}) async-start(bf16[64,2,1280]{2,1,0:T(2,128)(2,1)} %shard_map.65), calls=%async_computation.1 | async-start | bytes 655360 | tf_op jit(solution)/shard_map/all_to_all | solution.py:208
  53.6 0.0 all-gather.2.cloned.1.call-start
  53.7 0.3 shard_map.66
  53.9 13.3 %all-to-all-done.1.in_ref = bf16[64,2,1280]{2,1,0:T(2,128)(2,1)S(1)} async-done(((bf16[64,2,1280]{2,1,0:T(2,128)(2,1)}), bf16[64,2,1280]{2,1,0:T(2,128)(2,1)S(1)}, u32[]{:S(2)}, u32[]{:S(2)}) %all-to-all-start.1) | async-done | bytes 327712 | tf_op jit(solution)/shard_map/all_to_all | solution.py:208
  67.2 0.2 broadcast_in_dim.2
  67.5 1.2 shard_map.67
  68.7 0.0 all-gather.2.cloned.1.call-update
  68.7 34.6 %all_to_all.15 = bf16[16,320,128]{2,1,0:T(8,128)(2,1)S(1)} all-to-all(bf16[16,320,128]{2,1,0:T(8,128)(2,1)S(1)} %broadcast_in_dim.2), channel_id=1, replica_groups=mesh['z'=8,'yh'=4,'core'=2,'yl'=2,'x'=8] {'yl','x'}, dimensions={0} | all-to-all | bytes 2621440 | tf_op jit(solution)/shard_map/all_to_all | solution.py:214
  103.4 2.9 %shard_map.68.left_ref = bf16[2,320,2048]{2,1,0:T(8,128)(2,1)S(1)} custom-call(bf16[5120,128]{1,0:T(8,128)(2,1)S(1)} %bitcast.4), custom_call_target="tpu_custom_call" | custom-call | tf_op jit(solution)/shard_map/pallas_call | solution.py:143
  106.3 0.0 all-gather.2.cloned.1.call-done.right_ref
  106.3 5.4 %collective-permute-start = (bf16[1024,1280]{1,0:T(8,128)(2,1)}, bf16[1024,1280]{1,0:T(8,128)(2,1)S(1)}, u32[]{:S(2)}, u32[]{:S(2)}) collective-permute-start(bf16[1024,1280]{1,0:T(8,128)(2,1)} %all-gather.2.cloned.1.call-done.right_ref), channel_id=1, source_target_pairs={{0,16},{16,0},{1,17},{17,1},{2,18},{18,2},{3,19},{19,3},{4,20},{20... | collective-permute-start | bytes 7864328 | tf_op jit(solution)/shard_map/ppermute | solution.py:219
  111.7 0.0 copy-start
  111.8 1.7 %copy-done = bf16[1024,1280]{1,0:T(8,128)(2,1)S(1)} copy-done((bf16[1024,1280]{1,0:T(8,128)(2,1)S(1)}, bf16[1024,1280]{1,0:T(8,128)(2,1)}, u32[]{:S(2)}) %copy-start) | copy-done | bytes 2621464
  113.5 2.9 %shard_map.69.refs_0_ = f32[2,320,1280]{2,1,0:T(8,128)S(1)} custom-call(s32[1]{0:T(128)} %bitcast.half_ref, bf16[2,320,2048]{2,1,0:T(8,128)(2,1)S(1)} %shard_map.68.left_ref, bf16[1024,1280]{1,0:T(8,128)(2,1)S(1)} %copy-done), custom_call_target="tpu_custom_call" | custom-call | flops 1677721600 | bytes 7208960 | tf_op jit(solution)/shard_map/pallas_call | solution.py:168
  116.4 0.1 collective-permute-done.right_ref
  116.5 4.1 %shard_map.70 = f32[2,320,1280]{2,1,0:T(8,128)} custom-call(s32[1]{0:T(128)S(6)} %sub.3.half_ref, bf16[2,320,2048]{2,1,0:T(8,128)(2,1)S(1)} %shard_map.68.left_ref, bf16[1024,1280]{1,0:T(8,128)(2,1)S(1)} %collective-permute-done.right_ref, f32[2,320,1280]{2,1,0:T(8,128)S(1)} %shard_map.69.refs_0_), custom_call_target="tpu_custom_call" | custom-call | flops 1677721600 | bytes 7208960 | tf_op jit(solution)/shard_map/pallas_call | solution.py:168
Async XLA Ops:
  8.4 36.4 %all-to-all-start = ((bf16[64,2,384]{2,1,0:T(2,128)(2,1)}), bf16[64,2,384]{2,1,0:T(2,128)(2,1)S(1)}, u32[]{:S(2)}, u32[]{:S(2)}) async-start(bf16[64,2,384]{2,1,0:T(2,128)(2,1)} %shard_map.64), calls=%async_computation | async-start | bytes 196608 | tf_op jit(solution)/shard_map/all_to_all | solution.py:205
  44.8 22.4 %all-to-all-start.1 = ((bf16[64,2,1280]{2,1,0:T(2,128)(2,1)}), bf16[64,2,1280]{2,1,0:T(2,128)(2,1)S(1)}, u32[]{:S(2)}, u32[]{:S(2)}) async-start(bf16[64,2,1280]{2,1,0:T(2,128)(2,1)} %shard_map.65), calls=%async_computation.1 | async-start | bytes 655360 | tf_op jit(solution)/shard_map/all_to_all | solution.py:208
  53.6 52.7 %all-gather.2.cloned.1.call-start = ((), (), s32[]{:S(2)}) async-start(), calls=%async_computation.3 | async-start | bytes 2949120 | tf_op jit(solution)/shard_map/all_gather | solution.py:215
  106.3 10.2 %collective-permute-start = (bf16[1024,1280]{1,0:T(8,128)(2,1)}, bf16[1024,1280]{1,0:T(8,128)(2,1)S(1)}, u32[]{:S(2)}, u32[]{:S(2)}) collective-permute-start(bf16[1024,1280]{1,0:T(8,128)(2,1)} %all-gather.2.cloned.1.call-done.right_ref), channel_id=1, source_target_pairs={{0,16},{16,0},{1,17},{17,1},{2,18},{18,2},{3,19},{19,3},{4,20},{20... | collective-permute-start | bytes 7864328 | tf_op jit(solution)/shard_map/ppermute | solution.py:219
  111.7 1.7 %copy-start = (bf16[1024,1280]{1,0:T(8,128)(2,1)S(1)}, bf16[1024,1280]{1,0:T(8,128)(2,1)}, u32[]{:S(2)}) copy-start(bf16[1024,1280]{1,0:T(8,128)(2,1)} %all-gather.2.cloned.1.call-done.right_ref) | copy-start | bytes 7864324
Sparse Core Ops, SparseCore 0:
  68.8 36.9 all-gather.1

commit v6 on v5

--- a/solution.py
+++ b/solution.py
@@ -18,18 +18,16 @@
 WHOLE = pltpu.CompilerParams(vmem_limit_bytes=60 * 1024 * 1024)
 
 
-def split_right(elems, n_col, copies):
+def split_right(elems, n_col):
     width = elems.shape[2] // n_col
 
     def kernel(in_ref, out_ref):
         for block in range(n_col):
-            part = in_ref[0, :, block * width : (block + 1) * width]
-            for copy in range(copies):
-                out_ref[copy * n_col + block] = part
-
-    return pl.pallas_call(
-        kernel,
-        out_shape=jax.ShapeDtypeStruct((copies * n_col, 2, width), BF16),
+            out_ref[block] = in_ref[0, :, block * width : (block + 1) * width]
+
+    return pl.pallas_call(
+        kernel,
+        out_shape=jax.ShapeDtypeStruct((n_col, 2, width), BF16),
         in_specs=[VMEM],
         out_specs=VMEM,
         compiler_params=WHOLE,
@@ -62,23 +60,27 @@
     )(position, *tables, elems)
 
 
-def part_rows(slots):
-    count, _, width = slots.shape
-
-    def kernel(in_ref, out_ref):
+def part_rows(groups):
+    count, _, width = groups[0].shape
+    total = len(groups) * count
+
+    def kernel(*refs):
+        out_ref = refs[-1]
         for tile in range(width // LANES):
             cut = slice(tile * LANES, (tile + 1) * LANES)
-            both = in_ref[:, :, cut].astype(F32)
-            out_ref[:count, cut] = both[:, 0, :].astype(BF16)
-            out_ref[count:, cut] = both[:, 1, :].astype(BF16)
-
-    return pl.pallas_call(
-        kernel,
-        out_shape=jax.ShapeDtypeStruct((2 * count, width), BF16),
-        in_specs=[VMEM],
+            for place, in_ref in enumerate(refs[:-1]):
+                both = in_ref[:, :, cut].astype(F32)
+                at = place * count
+                out_ref[at : at + count, cut] = both[:, 0, :].astype(BF16)
+                out_ref[total + at : total + at + count, cut] = both[:, 1, :].astype(BF16)
+
+    return pl.pallas_call(
+        kernel,
+        out_shape=jax.ShapeDtypeStruct((2 * total, width), BF16),
+        in_specs=[VMEM] * len(groups),
         out_specs=VMEM,
         compiler_params=LIMIT,
-    )(slots)
+    )(*groups)
 
 
 def pack_left(slots, shift):
@@ -109,7 +111,7 @@
     )(shift, slots)
 
 
-def order_left(slabs, n_row, n_col, n_far, width):
+def order_left(here, slabs, n_row, n_col, n_far, width):
     group = n_row // n_far
     near = n_far * n_col
     depth = 2 * n_row * n_col
@@ -117,15 +119,16 @@
     slots = 5 * n_row
     step = 2 * near
 
-    def kernel(in_ref, out_ref, rows_ref):
+    def kernel(here_ref, in_ref, out_ref, rows_ref):
         for col in range(n_col):
             for far in range(n_far):
+                held = lax.rem(here_ref[0] + far, n_far)
                 first = pl.ds(far * n_col + col, group, stride=step)
                 second = pl.ds(near + far * n_col + col, group, stride=step)
                 rows = []
                 for slab in range(5):
-                    at = col * slots + slab * n_row + far * group
-                    rows.append(in_ref[at : at + group, :].astype(F32))
+                    at = pl.multiple_of(col * slots + slab * n_row + held * group, group)
+                    rows.append(in_ref[pl.ds(at, group), :].astype(F32))
                 rows = [(rows[0], rows[2]), (rows[1], rows[3]), (rows[4], pltpu.roll(rows[4], half, 1))]
                 for tile, (re, im) in enumerate(rows):
                     rows_ref[tile, first, :] = re
@@ -143,11 +146,11 @@
     return pl.pallas_call(
         kernel,
         out_shape=jax.ShapeDtypeStruct((2, width, depth), BF16),
-        in_specs=[VMEM],
+        in_specs=[SMEM, VMEM],
         out_specs=VMEM,
         scratch_shapes=[pltpu.VMEM((3, depth, LANES), F32)],
         compiler_params=LIMIT,
-    )(slabs)
+    )(here, slabs)
 
 
 def multiply(half, left, right, total=None):
@@ -200,20 +203,26 @@
         z, far, side = block // (2 * n_far), block // 2 % n_far, block % 2
         return (far * 2 + side) * n_z + z
 
+    right = split_right(pair_elems, n_col)
+    right = lax.all_to_all(right, COL, split_axis=0, concat_axis=0, tiled=True)
+
     tables = (slot_pair, val_index, cond_index, val_energy, cond_energy)
     left = split_left(pair_elems, tables, position, n_row, span, place_of)
+    left, right = lax.optimization_barrier((left, right))
+    groups = [right]
+    for step in range(1, n_far):
+        groups.append(lax.ppermute(right, "yh", [(far, (far - step) % n_far) for far in range(n_far)]))
     left = lax.all_to_all(left, ("yh", "core", "z"), split_axis=0, concat_axis=0, tiled=True)
-    right = split_right(pair_elems, n_col, n_far)
-    left, right = lax.optimization_barrier((left, right))
-    right = lax.all_to_all(right, ("yh", *COL), split_axis=0, concat_axis=0, tiled=True)
+    left, groups = lax.optimization_barrier((left, groups))
 
     shift = lax.rem(row * width, LANES).astype(jnp.int32).reshape(1)
     left = pack_left(left, shift)
     left = jnp.broadcast_to(left[None], (n_col, *left.shape))
-    right, left = lax.optimization_barrier((right, left))
+    right, left = lax.optimization_barrier((part_rows(groups), left))
     left = lax.all_to_all(left, COL, split_axis=0, concat_axis=0, tiled=True)
-    right = lax.all_gather(part_rows(right), "z", axis=0, tiled=True)
-    left = order_left(left.reshape(n_col * left.shape[1], LANES), n_row, n_col, n_far, width)
+    right = lax.all_gather(right, "z", axis=0, tiled=True)
+    here = lax.axis_index("yh").astype(jnp.int32).reshape(1)
+    left = order_left(here, left.reshape(n_col * left.shape[1], LANES), n_row, n_col, n_far, width)
     right, left = lax.optimization_barrier((right, left))
 
     other = lax.ppermute(right, "core", [(0, 1), (1, 0)])

time: 128 us -> 133 us (1.039)
  starting transfers between devices: 38.7 us -> 53.1 us
  waiting for transfers between devices: 23.7 us -> 15 us
    ppermute x0 -> x3, starting transfers between devices: none -> 14.7 us  [local(): lax.ppermute(right, 'yh', [(far, (far - step) % n_far) for far in range(n...]
    all_to_all x1, waiting for transfers between devices: 10.3 us -> 0.01 us  [local(): lax.all_to_all(left, ('yh', 'core', 'z'), split_axis=0, concat_axis=0, ti...]
    all_to_all x1, waiting for transfers between devices: 13.3 us -> 5.51 us  [local(): right = lax.all_to_all(right, COL, split_axis=0, concat_axis=0, tiled=True)]
    all_gather x1, waiting for transfers between devices: 0.02 us -> 6.01 us  [local(): right = lax.all_gather(right, 'z', axis=0, tiled=True)]
    ppermute x0 -> x3, waiting for transfers between devices: none -> 3.37 us  [local(): lax.ppermute(right, 'yh', [(far, (far - step) % n_far) for far in range(n...]
  transfers between devices with their start and end apart: 4 -> 7, of which waited for: 3 -> 5; matrix products, arithmetic and copies ran while one was open for 0% -> 0% of each run, Pallas kernels for 6% -> 6%
where the time goes in v6:
time: 133 us; the launch traced here: 132 us
  starting transfers between devices  53.1 us (40%)
  blocking collectives  33.5 us (25%)
  waiting for transfers between devices  15 us (11%)
  Pallas kernels  14.9 us (11%)
  between operations  13.5 us (10%)
  local copies, waits for them, and re-layouts  1.98 us (1%)
    all_to_all x1, blocking collectives, local(): left = lax.all_to_all(left, COL, split_axis=0, concat_axis=0, tiled=True)  33.5 us
    all_to_all x1, starting transfers between devices, local(): lax.all_to_all(left, ('yh', 'core', 'z'), split_axis=0, concat_axis=0, ti...  24.2 us
    ppermute x3, starting transfers between devices, local(): lax.ppermute(right, 'yh', [(far, (far - step) % n_far) for far in range(n...  14.7 us
    all_to_all x1, starting transfers between devices, local(): right = lax.all_to_all(right, COL, split_axis=0, concat_axis=0, tiled=True)  8.54 us
    pallas_call x2, Pallas kernels, multiply(): pl.pallas_call(kernel, grid_spec=pltpu.PrefetchScalarGridSpec(num_scalar_...  7.02 us
    all_gather x1, waiting for transfers between devices, local(): right = lax.all_gather(right, 'z', axis=0, tiled=True)  6.01 us
    ppermute x1, starting transfers between devices, local(): other = lax.ppermute(right, 'core', [(0, 1), (1, 0)])  5.67 us
    all_to_all x1, waiting for transfers between devices, local(): right = lax.all_to_all(right, COL, split_axis=0, concat_axis=0, tiled=True)  5.51 us
  transfers between devices with their start and end apart: 7, of which 5 were waited for; matrix products, arithmetic and copies ran while one was open for 0% of the time, Pallas kernels for 6%

profile of v6, /device:TPU:1, one launch (start us, length us, event | category | flops | bytes accessed | tf_op | source)
XLA Modules:
  0.0 132.0 jit_solution(10647842799937959673)
XLA Ops:
  6.5 1.5 %shard_map.65 = bf16[16,2,1280]{2,1,0:T(2,128)(2,1)} custom-call(bf16[1,2,20480]{2,1,0:T(2,128)(2,1)} %in_ref.3), custom_call_target="tpu_custom_call" | custom-call | tf_op jit(solution)/shard_map/pallas_call | solution.py:28
  8.1 8.5 %all-to-all-start = ((bf16[16,2,1280]{2,1,0:T(2,128)(2,1)}), bf16[16,2,1280]{2,1,0:T(2,128)(2,1)S(1)}, u32[]{:S(2)}, u32[]{:S(2)}) async-start(bf16[16,2,1280]{2,1,0:T(2,128)(2,1)} %shard_map.65), calls=%async_computation | async-start | bytes 163840 | tf_op jit(solution)/shard_map/all_to_all | solution.py:207
  16.6 1.9 %shard_map.64 = bf16[64,2,384]{2,1,0:T(2,128)(2,1)} custom-call(s32[1]{0:T(128)} %bitcast.1.where_ref, s32[1024]{0:T(1024)} %slot_ref.1, s32[1024]{0:T(1024)} %val_ref.1, s32[1024]{0:T(1024)} %cond_ref.1, f32[2048]{0:T(1024)} %upper_ref.1, f32[2048]{0:T(1024)} %lower_ref.1, bf16[1,2,20480]{2,1,0:T(2,128)(2,1)} %in_ref.3), custom_call_target="tpu_custom_call" | custom-call | tf_op jit(solution)/shard_map/pallas_call | solution.py:54
  18.5 5.5 %all-to-all-done.refs_0_ = bf16[16,2,1280]{2,1,0:T(2,128)(2,1)S(1)} async-done(((bf16[16,2,1280]{2,1,0:T(2,128)(2,1)}), bf16[16,2,1280]{2,1,0:T(2,128)(2,1)S(1)}, u32[]{:S(2)}, u32[]{:S(2)}) %all-to-all-start) | async-done | bytes 81952 | tf_op jit(solution)/shard_map/all_to_all | solution.py:207
  24.0 24.2 %all-to-all-start.1 = ((bf16[64,2,384]{2,1,0:T(2,128)(2,1)}), bf16[64,2,384]{2,1,0:T(2,128)(2,1)S(1)}, u32[]{:S(2)}, u32[]{:S(2)}) async-start(bf16[64,2,384]{2,1,0:T(2,128)(2,1)} %shard_map.64), calls=%async_computation.1 | async-start | bytes 196608 | tf_op jit(solution)/shard_map/all_to_all | solution.py:215
  48.2 0.0 all-gather.2.cloned.1.call-start
  48.2 4.2 %collective-permute-start.2 = (bf16[16,2,1280]{2,1,0:T(2,128)(2,1)S(1)}, bf16[16,2,1280]{2,1,0:T(2,128)(2,1)S(1)}, u32[]{:S(2)}, u32[]{:S(2)}) collective-permute-start(bf16[16,2,1280]{2,1,0:T(2,128)(2,1)S(1)} %all-to-all-done.refs_0_), channel_id=1, source_target_pairs={{0,32},{32,64},{64,96},{96,0},{1,33},{33,65},{65,97},{97,1},{2,34}... | collective-permute-start | bytes 245768 | tf_op jit(solution)/shard_map/ppermute | solution.py:214
  52.4 5.4 %collective-permute-start.1 = (bf16[16,2,1280]{2,1,0:T(2,128)(2,1)S(1)}, bf16[16,2,1280]{2,1,0:T(2,128)(2,1)S(1)}, u32[]{:S(2)}, u32[]{:S(2)}) collective-permute-start(bf16[16,2,1280]{2,1,0:T(2,128)(2,1)S(1)} %all-to-all-done.refs_0_), channel_id=1, source_target_pairs={{0,64},{32,96},{64,0},{96,32},{1,65},{33,97},{65,1},{97,33},{2,66}... | collective-permute-start | bytes 245768 | tf_op jit(solution)/shard_map/ppermute | solution.py:214
  57.8 5.1 %collective-permute-start = (bf16[16,2,1280]{2,1,0:T(2,128)(2,1)S(1)}, bf16[16,2,1280]{2,1,0:T(2,128)(2,1)S(1)}, u32[]{:S(2)}, u32[]{:S(2)}) collective-permute-start(bf16[16,2,1280]{2,1,0:T(2,128)(2,1)S(1)} %all-to-all-done.refs_0_), channel_id=1, source_target_pairs={{0,96},{32,0},{64,32},{96,64},{1,97},{33,1},{65,33},{97,65},{2,98}... | collective-permute-start | bytes 245768 | tf_op jit(solution)/shard_map/ppermute | solution.py:214
  63.0 0.0 collective-permute-done.2.refs_3_
  63.0 1.6 %collective-permute-done.1.refs_2_ = bf16[16,2,1280]{2,1,0:T(2,128)(2,1)S(1)} collective-permute-done((bf16[16,2,1280]{2,1,0:T(2,128)(2,1)S(1)}, bf16[16,2,1280]{2,1,0:T(2,128)(2,1)S(1)}, u32[]{:S(2)}, u32[]{:S(2)}) %collective-permute-start.1) | collective-permute-done | bytes 81952 | tf_op jit(solution)/shard_map/ppermute | solution.py:214
  64.5 1.8 %collective-permute-done.refs_1_ = bf16[16,2,1280]{2,1,0:T(2,128)(2,1)S(1)} collective-permute-done((bf16[16,2,1280]{2,1,0:T(2,128)(2,1)S(1)}, bf16[16,2,1280]{2,1,0:T(2,128)(2,1)S(1)}, u32[]{:S(2)}, u32[]{:S(2)}) %collective-permute-start) | collective-permute-done | bytes 81952 | tf_op jit(solution)/shard_map/ppermute | solution.py:214
  66.3 0.0 all-to-all-done.1.in_ref
  66.3 0.3 shard_map.67
  66.6 1.1 shard_map.66
  67.8 0.2 broadcast_in_dim.2
  68.0 0.0 all-gather.2.cloned.1.call-update
  68.0 33.5 %all_to_all.15 = bf16[16,320,128]{2,1,0:T(8,128)(2,1)S(1)} all-to-all(bf16[16,320,128]{2,1,0:T(8,128)(2,1)S(1)} %broadcast_in_dim.2), channel_id=1, replica_groups=mesh['z'=8,'yh'=4,'core'=2,'yl'=2,'x'=8] {'yl','x'}, dimensions={0} | all-to-all | bytes 2621440 | tf_op jit(solution)/shard_map/all_to_all | solution.py:222
  101.6 3.0 %shard_map.68.left_ref = bf16[2,320,2048]{2,1,0:T(8,128)(2,1)S(1)} custom-call(s32[1]{0:T(128)} %bitcast.3.here_ref, bf16[5120,128]{1,0:T(8,128)(2,1)S(1)} %bitcast.5), custom_call_target="tpu_custom_call" | custom-call | tf_op jit(solution)/shard_map/pallas_call | solution.py:146
  104.6 6.0 %all-gather.2.cloned.1.call-done.right_ref = bf16[1024,1280]{1,0:T(8,128)(2,1)} async-done(((bf16[128,1280]{1,0:T(8,128)(2,1)}), bf16[1024,1280]{1,0:T(8,128)(2,1)}) %all-gather.2.cloned.1.call-update) | async-done | bytes 2621456 | tf_op jit(solution)/shard_map/all_gather | solution.py:223
  110.6 5.7 %collective-permute-start.3 = (bf16[1024,1280]{1,0:T(8,128)(2,1)}, bf16[1024,1280]{1,0:T(8,128)(2,1)S(1)}, u32[]{:S(2)}, u32[]{:S(2)}) collective-permute-start(bf16[1024,1280]{1,0:T(8,128)(2,1)} %all-gather.2.cloned.1.call-done.right_ref), channel_id=1, source_target_pairs={{0,16},{16,0},{1,17},{17,1},{2,18},{18,2},{3,19},{19,3},{4,20},{20... | collective-permute-start | bytes 7864328 | tf_op jit(solution)/shard_map/ppermute | solution.py:228
  116.3 0.0 copy-start
  116.3 1.7 %copy-done = bf16[1024,1280]{1,0:T(8,128)(2,1)S(1)} copy-done((bf16[1024,1280]{1,0:T(8,128)(2,1)S(1)}, bf16[1024,1280]{1,0:T(8,128)(2,1)}, u32[]{:S(2)}) %copy-start) | copy-done | bytes 2621464
  118.1 2.9 %shard_map.69.refs_0_ = f32[2,320,1280]{2,1,0:T(8,128)S(1)} custom-call(s32[1]{0:T(128)} %bitcast.half_ref, bf16[2,320,2048]{2,1,0:T(8,128)(2,1)S(1)} %shard_map.68.left_ref, bf16[1024,1280]{1,0:T(8,128)(2,1)S(1)} %copy-done), custom_call_target="tpu_custom_call" | custom-call | flops 1677721600 | bytes 7208960 | tf_op jit(solution)/shard_map/pallas_call | solution.py:171
  121.0 0.1 collective-permute-done.3.right_ref
  121.0 4.1 %shard_map.70 = f32[2,320,1280]{2,1,0:T(8,128)} custom-call(s32[1]{0:T(128)S(6)} %sub.3.half_ref, bf16[2,320,2048]{2,1,0:T(8,128)(2,1)S(1)} %shard_map.68.left_ref, bf16[1024,1280]{1,0:T(8,128)(2,1)S(1)} %collective-permute-done.3.right_ref, f32[2,320,1280]{2,1,0:T(8,128)S(1)} %shard_map.69.refs_0_), custom_call_target="tpu_custom_call" | custom-call | flops 1677721600 | bytes 7208960 | tf_op jit(solution)/shard_map/pallas_call | solution.py:171
Async XLA Ops:
  8.1 15.9 %all-to-all-start = ((bf16[16,2,1280]{2,1,0:T(2,128)(2,1)}), bf16[16,2,1280]{2,1,0:T(2,128)(2,1)S(1)}, u32[]{:S(2)}, u32[]{:S(2)}) async-start(bf16[16,2,1280]{2,1,0:T(2,128)(2,1)} %shard_map.65), calls=%async_computation | async-start | bytes 163840 | tf_op jit(solution)/shard_map/all_to_all | solution.py:207
  24.0 42.3 %all-to-all-start.1 = ((bf16[64,2,384]{2,1,0:T(2,128)(2,1)}), bf16[64,2,384]{2,1,0:T(2,128)(2,1)S(1)}, u32[]{:S(2)}, u32[]{:S(2)}) async-start(bf16[64,2,384]{2,1,0:T(2,128)(2,1)} %shard_map.64), calls=%async_computation.1 | async-start | bytes 196608 | tf_op jit(solution)/shard_map/all_to_all | solution.py:215
  48.2 62.5 %all-gather.2.cloned.1.call-start = ((), (), s32[]{:S(2)}) async-start(), calls=%async_computation.3 | async-start | bytes 2949120 | tf_op jit(solution)/shard_map/all_gather | solution.py:223
  48.2 14.7 %collective-permute-start.2 = (bf16[16,2,1280]{2,1,0:T(2,128)(2,1)S(1)}, bf16[16,2,1280]{2,1,0:T(2,128)(2,1)S(1)}, u32[]{:S(2)}, u32[]{:S(2)}) collective-permute-start(bf16[16,2,1280]{2,1,0:T(2,128)(2,1)S(1)} %all-to-all-done.refs_0_), channel_id=1, source_target_pairs={{0,32},{32,64},{64,96},{96,0},{1,33},{33,65},{65,97},{97,1},{2,34}... | collective-permute-start | bytes 245768 | tf_op jit(solution)/shard_map/ppermute | solution.py:214
  52.4 12.1 %collective-permute-start.1 = (bf16[16,2,1280]{2,1,0:T(2,128)(2,1)S(1)}, bf16[16,2,1280]{2,1,0:T(2,128)(2,1)S(1)}, u32[]{:S(2)}, u32[]{:S(2)}) collective-permute-start(bf16[16,2,1280]{2,1,0:T(2,128)(2,1)S(1)} %all-to-all-done.refs_0_), channel_id=1, source_target_pairs={{0,64},{32,96},{64,0},{96,32},{1,65},{33,97},{65,1},{97,33},{2,66}... | collective-permute-start | bytes 245768 | tf_op jit(solution)/shard_map/ppermute | solution.py:214
  57.8 8.5 %collective-permute-start = (bf16[16,2,1280]{2,1,0:T(2,128)(2,1)S(1)}, bf16[16,2,1280]{2,1,0:T(2,128)(2,1)S(1)}, u32[]{:S(2)}, u32[]{:S(2)}) collective-permute-start(bf16[16,2,1280]{2,1,0:T(2,128)(2,1)S(1)} %all-to-all-done.refs_0_), channel_id=1, source_target_pairs={{0,96},{32,0},{64,32},{96,64},{1,97},{33,1},{65,33},{97,65},{2,98}... | collective-permute-start | bytes 245768 | tf_op jit(solution)/shard_map/ppermute | solution.py:214
  110.6 10.4 %collective-permute-start.3 = (bf16[1024,1280]{1,0:T(8,128)(2,1)}, bf16[1024,1280]{1,0:T(8,128)(2,1)S(1)}, u32[]{:S(2)}, u32[]{:S(2)}) collective-permute-start(bf16[1024,1280]{1,0:T(8,128)(2,1)} %all-gather.2.cloned.1.call-done.right_ref), channel_id=1, source_target_pairs={{0,16},{16,0},{1,17},{17,1},{2,18},{18,2},{3,19},{19,3},{4,20},{20... | collective-permute-start | bytes 7864328 | tf_op jit(solution)/shard_map/ppermute | solution.py:228
  116.3 1.7 %copy-start = (bf16[1024,1280]{1,0:T(8,128)(2,1)S(1)}, bf16[1024,1280]{1,0:T(8,128)(2,1)}, u32[]{:S(2)}) copy-start(bf16[1024,1280]{1,0:T(8,128)(2,1)} %all-gather.2.cloned.1.call-done.right_ref) | copy-start | bytes 7864324
Sparse Core Ops, SparseCore 0:
  68.2 42.4 all-gather.1
